TPU v7x, 256 devices: a whole 4x4x8 slice. The times are simulated.
256 devices in a mesh: fsdp: 16 (over x_lo, z), st: 16 (over y, x_hi, core).
Axes of the slice: x: 4 (x_hi: 2, x_lo: 2; x = x_hi * 2 + x_lo), y: 4, z: 8, core: 2. Of those that a mesh axis runs over, the one named last changes fastest.
Arguments:
- queries: bfloat16 [1, 24576, 2048], P(None, 'st', 'fsdp'), may hold values from -4.5 to 4.5
- key_rows: bfloat16 [1, 24576, 2048], P(None, 'st', 'fsdp'), may hold values from -4.5 to 4.5
- value_rows: bfloat16 [1, 24576, 2048], P(None, 'st', 'fsdp'), may hold values from -6 to 6
- out_grad: bfloat16 [1, 24576, 1536], P(None, 'st', 'fsdp'), may hold values from -6 to 6
- proj_weight: bfloat16 [2048, 1536], P('fsdp'), may hold values from -0.125 to 0.125
- pattern: int32 [64, 27], P('st'), may hold values from -1 to 63, as said below
Outputs:
- projected: bfloat16 [1, 24576, 1536], P(None, 'st', 'fsdp')
- query_grad: bfloat16 [1, 24576, 2048], P(None, 'st', 'fsdp')
- key_grad: bfloat16 [1, 24576, 2048], P(None, 'st', 'fsdp')
- value_grad: bfloat16 [1, 24576, 2048], P(None, 'st', 'fsdp')
- weight_grad: float32 [2048, 1536], P('fsdp', 'st')
Inputs may be any that keep to these rules, and one draw needn't show every extreme that they name: Slot j stands for the offsets (j // 9 - 1) in frame, (j // 3 % 3 - 1) in tile row and (j % 3 - 1) in column; pattern[t, j] is -1 or the tile at t's frame, row and column plus those offsets, which lies inside the grid of 2 frames, 16 rows and 2 columns; slots 10, 13 and 16 are never -1 where that tile exists.
All inputs are finite; a program needn't handle non-finite values.
Results may differ from a plain program's by a relative error of at most 0.023.
Values may be sent and summed in bfloat16 or wider, within the bound.
No kernel may reach another device: no remote copies, remote signals or barrier semaphores. Data moves between devices by JAX's collectives and lax.ppermute only.
A program may use at most 128 MiB of HBM per device.

v0:
```python
import functools

import jax
import jax.numpy as jnp
from jax import lax
from jax.experimental import pallas as pl
from jax.experimental.pallas import tpu as pltpu
from jax.sharding import Mesh
from jax.sharding import PartitionSpec as P

HDIM = 128
TILE = 384
TF = 2
TC = 2
ROW_TILES = TF * TC
BAND = 3 * ROW_TILES
SCALING = HDIM ** (-0.5)
LOG2E = 1.4426950408889634
BF = jnp.bfloat16
F32 = jnp.float32
ST = ("y", "xh", "core")
NT = (((1,), (1,)), ((), ()))
TN = (((0,), (0,)), ((), ()))
NN = (((1,), (0,)), ((), ()))


def dot(a, b, dims):
    return lax.dot_general(a, b, dims, preferred_element_type=F32)


def build_pairs(pattern_ref, tile_of, place_of, rows):
    count = jnp.int32(0)
    for tile in range(ROW_TILES):
        frame, col = tile // TC, tile % TC
        for at, row in enumerate(rows):
            for inner in range(ROW_TILES):
                slot = (inner // TC - frame + 1) * 9 + row * 3 + (inner % TC - col + 1)
                tile_of[count] = jnp.int32(tile)
                place_of[count] = jnp.int32(at * ROW_TILES + inner)
                count = count + (pattern_ref[tile, slot] >= 0).astype(jnp.int32)
    return count


def run_pairs(count, make, use, even, odd):
    make(even, 0)

    def step(j, carry):
        i = 2 * j
        make(odd, i + 1)
        use(even, i)
        make(even, i + 2)
        use(odd, i + 1)
        return carry

    lax.fori_loop(0, (count - 1) // 2, step, 0)

    @pl.when(count % 2 == 1)
    def _():
        use(even, count - 1)

    @pl.when(count % 2 == 0)
    def _():
        make(odd, count - 1)
        use(even, count - 2)
        use(odd, count - 1)


def fill_band(refs, kband, vband, sem):
    copies = []
    for i, ref in enumerate(refs):
        place = pl.ds(i * ROW_TILES, ROW_TILES)
        copies.append(pltpu.make_async_copy(ref.at[0], kband.at[place], sem.at[2 * i]))
        copies.append(pltpu.make_async_copy(ref.at[1], vband.at[place], sem.at[2 * i + 1]))
    for copy in copies:
        copy.start()
    return copies


def forward_pairs(count, q_ref, kband, vband, tile_of, place_of, even, odd, top, total, acc):
    def make(slot, i):
        scores = dot(kband[place_of[i]], q_ref[tile_of[i]], NT) * (SCALING * LOG2E)
        slot[0][...] = scores
        slot[1][...] = jnp.max(scores, axis=0, keepdims=True)

    def use(slot, i):
        tile = tile_of[i]
        before = top[tile]
        peak = jnp.maximum(before, slot[1][...])
        shrink = jnp.exp2(before - peak)
        raised = jnp.exp2(slot[0][...] - peak)
        top[tile] = peak
        total[tile] = shrink * total[tile] + jnp.sum(raised, axis=0, keepdims=True)
        acc[tile] = shrink * acc[tile] + dot(vband[place_of[i]], raised.astype(BF), TN)

    run_pairs(count, make, use, even, odd)


def forward_own_kernel(
    pattern_ref, q_ref, k_ref, v_ref, top, total, acc, tile_of, place_of, s0, s1, m0, m1
):
    count = build_pairs(pattern_ref, tile_of, place_of, (1,))
    top[...] = jnp.full(top.shape, -jnp.inf, F32)
    total[...] = jnp.zeros(total.shape, F32)
    acc[...] = jnp.zeros(acc.shape, F32)
    forward_pairs(
        count, q_ref, k_ref, v_ref, tile_of, place_of, (s0, m0), (s1, m1), top, total, acc
    )


def forward_halo_kernel(
    pattern_ref, q_ref, top_in, total_in, acc_in, above_ref, below_ref, early_ref,
    att_ref, flip_ref, lse_ref,
    kband, vband, tile_of, place_of, s0, s1, m0, m1, top, total, acc, sem,
):
    copies = fill_band((above_ref, below_ref), kband, vband, sem)
    count = build_pairs(pattern_ref, tile_of, place_of, (0, 2))
    top[...] = top_in[...]
    total[...] = total_in[...]
    acc[...] = acc_in[...]
    for copy in copies:
        copy.wait()
    forward_pairs(
        count, q_ref, kband, vband, tile_of, place_of, (s0, m0), (s1, m1), top, total, acc
    )
    for tile in range(ROW_TILES):
        attended = acc[tile] / total[tile]
        flip_ref[tile] = attended.astype(BF)
        att_ref[tile] = attended.T.astype(BF)
        lse_ref[tile] = top[tile] + jnp.log2(total[tile])


def backward_pairs(
    count, q_ref, back, att_ref, lse_ref, kband, vband, tile_of, place_of,
    even, odd, delta, dk, dv, dq,
):
    for tile in range(ROW_TILES):
        prod = back[tile].astype(F32) * att_ref[tile].astype(F32)
        delta[tile] = jnp.sum(prod, axis=0, keepdims=True)

    def make(slot, i):
        tile, place = tile_of[i], place_of[i]
        scores = dot(kband[place], q_ref[tile], NT) * (SCALING * LOG2E)
        prob = jnp.exp2(scores - lse_ref[tile])
        prob_grad = dot(vband[place], back[tile], NN)
        slot[0][...] = prob.astype(BF)
        slot[1][...] = (prob * (prob_grad - delta[tile])).astype(BF)

    def use(slot, i):
        tile, place = tile_of[i], place_of[i]
        dv[place] += dot(slot[0][...], back[tile], NT)
        dk[place] += dot(slot[1][...], q_ref[tile], NN)
        dq[tile] += dot(kband[place], slot[1][...], TN)

    run_pairs(count, make, use, even, odd)


def backward_halo_kernel(
    pattern_ref, q_ref, back_mine_ref, back_got_ref, att_ref, lse_ref, above_ref, below_ref,
    early_ref,
    up_ref, down_ref, dq, back_ref, zero_ref,
    kband, vband, tile_of, place_of, p0, p1, d0, d1, delta, dk, dv, sem,
):
    copies = fill_band((above_ref, below_ref), kband, vband, sem)
    count = build_pairs(pattern_ref, tile_of, place_of, (0, 2))
    dk[...] = jnp.zeros(dk.shape, F32)
    dv[...] = jnp.zeros(dv.shape, F32)
    dq[...] = jnp.zeros(dq.shape, F32)
    zero_ref[...] = jnp.zeros(zero_ref.shape, F32)
    for tile in range(ROW_TILES):
        cols = pl.ds(tile * TILE, TILE)
        back_ref[tile] = (back_mine_ref[:, cols] + back_got_ref[:, cols].astype(F32)).astype(BF)
    for copy in copies:
        copy.wait()
    backward_pairs(
        count, q_ref, back_ref, att_ref, lse_ref, kband, vband, tile_of, place_of,
        (p0, d0), (p1, d1), delta, dk, dv, dq,
    )
    for i in range(ROW_TILES):
        up_ref[0, i] = dk[i].astype(BF)
        up_ref[1, i] = dv[i].astype(BF)
        down_ref[0, i] = dk[ROW_TILES + i].astype(BF)
        down_ref[1, i] = dv[ROW_TILES + i].astype(BF)


def backward_own_kernel(
    pattern_ref, q_ref, back_ref, att_ref, lse_ref, k_ref, v_ref, dq_in, early_ref,
    dq_ref, dk, dv, zero_ref,
    tile_of, place_of, p0, p1, d0, d1, delta, dq,
):
    count = build_pairs(pattern_ref, tile_of, place_of, (1,))
    dk[...] = jnp.zeros(dk.shape, F32)
    dv[...] = jnp.zeros(dv.shape, F32)
    zero_ref[...] = jnp.zeros(zero_ref.shape, F32)
    dq[...] = dq_in[...]
    backward_pairs(
        count, q_ref, back_ref, att_ref, lse_ref, k_ref, v_ref, tile_of, place_of,
        (p0, d0), (p1, d1), delta, dk, dv, dq,
    )
    for tile in range(ROW_TILES):
        dq_ref[tile] = (dq[tile] * SCALING).T.astype(BF)


def part_kernel(mine_ref, other_ref, att_ref, got_ref, early_ref, part_ref, weights, heads):
    weights[:HDIM] = mine_ref[...]
    weights[HDIM:] = other_ref[...]
    heads[:, :HDIM] = att_ref[...]
    heads[:, HDIM:] = got_ref[...]
    for tile in range(ROW_TILES):
        cols = slice(tile * TILE, (tile + 1) * TILE)
        terms = dot(weights[...], heads[cols], (((0,), (1,)), ((), ())))
        part_ref[:, cols] = terms.astype(BF)


def weight_kernel(place_ref, grad_ref, att_ref, other_ref, early_ref, send_ref, keep_ref, heads, total):
    half, core = place_ref[0], place_ref[1]
    heads[:, pl.ds(pl.multiple_of(half * HDIM, HDIM), HDIM)] = att_ref[...]
    heads[:, pl.ds(pl.multiple_of((1 - half) * HDIM, HDIM), HDIM)] = other_ref[...]
    total[...] = dot(grad_ref[...], heads[...], NN)
    rows = send_ref.shape[3]
    for low in range(2):
        for xh in range(2):
            chunk = low * 4 + xh * 2
            mine = pl.ds(pl.multiple_of((chunk + core) * rows, 8), rows)
            yours = pl.ds(pl.multiple_of((chunk + 1 - core) * rows, 8), rows)
            for a in range(2):
                lanes = slice(a * HDIM, (a + 1) * HDIM)
                keep_ref[a, low, xh] = total[mine, lanes]
                send_ref[a, low, xh] = total[yours, lanes].astype(BF)


VM = pl.BlockSpec(memory_space=pltpu.VMEM)
SM = pl.BlockSpec(memory_space=pltpu.SMEM)
HB = pl.BlockSpec(memory_space=pltpu.HBM)
BLOCK = (ROW_TILES, TILE, HDIM)
FLIP = (ROW_TILES, HDIM, TILE)
LINE = (ROW_TILES, 1, TILE)
HALO = (2 * ROW_TILES, TILE, HDIM)
PAIR_LISTS = [pltpu.SMEM((49,), jnp.int32), pltpu.SMEM((49,), jnp.int32)]
HALO_BAND = [pltpu.VMEM(HALO, BF), pltpu.VMEM(HALO, BF)]
SCORES = [pltpu.VMEM((TILE, TILE), F32)] * 2 + [pltpu.VMEM((1, TILE), F32)] * 2
TERMS = [pltpu.VMEM((TILE, TILE), BF)] * 4
DMA_SEMS = pltpu.SemaphoreType.DMA((4,))


def kernel_call(kernel, name, outs, in_specs, scratch, flops):
    return pl.pallas_call(
        kernel,
        name=name,
        out_shape=tuple(jax.ShapeDtypeStruct(shape, kind) for shape, kind in outs),
        in_specs=in_specs,
        out_specs=(VM,) * len(outs),
        scratch_shapes=scratch,
        compiler_params=pltpu.CompilerParams(vmem_limit_bytes=32 * 1024 * 1024),
        cost_estimate=pl.CostEstimate(
            flops=flops, bytes_accessed=4_000_000, transcendentals=3_000_000
        ),
    )


def forward_own(*args):
    return kernel_call(
        forward_own_kernel, "forward_own", [(LINE, F32), (LINE, F32), (FLIP, F32)],
        [SM, VM, VM, VM], PAIR_LISTS + SCORES, 3_000_000_000,
    )(*args)


def forward_halo(*args):
    state = [pltpu.VMEM(LINE, F32), pltpu.VMEM(LINE, F32), pltpu.VMEM(FLIP, F32)]
    return kernel_call(
        forward_halo_kernel, "forward_halo", [(BLOCK, BF), (FLIP, BF), (LINE, F32)],
        [SM] + [VM] * 4 + [HB] * 3, HALO_BAND + PAIR_LISTS + SCORES + state + [DMA_SEMS],
        5_000_000_000,
    )(*args)


def backward_halo(*args):
    outs = [((2,) + BLOCK, BF), ((2,) + BLOCK, BF), (FLIP, F32), (FLIP, BF), ((1, HDIM), F32)]
    return kernel_call(
        backward_halo_kernel, "backward_halo", outs, [SM] + [VM] * 5 + [HB] * 3,
        HALO_BAND + PAIR_LISTS + TERMS
        + [pltpu.VMEM(LINE, F32), pltpu.VMEM(HALO, F32), pltpu.VMEM(HALO, F32), DMA_SEMS],
        12_000_000_000,
    )(*args)


def backward_own(*args):
    outs = [(BLOCK, BF), (BLOCK, F32), (BLOCK, F32), ((1, HDIM), F32)]
    return kernel_call(
        backward_own_kernel, "backward_own", outs, [SM] + [VM] * 7 + [HB],
        PAIR_LISTS + TERMS + [pltpu.VMEM(LINE, F32), pltpu.VMEM(FLIP, F32)],
        6_000_000_000,
    )(*args)


def projected_part(w_mine, *args):
    feats, tokens = w_mine.shape[1], ROW_TILES * TILE
    return kernel_call(
        part_kernel, "projected_part", [((feats, tokens), BF)], [VM] * 4 + [HB],
        [pltpu.VMEM((2 * HDIM, feats), BF), pltpu.VMEM((tokens, 2 * HDIM), BF)], 2_000_000_000,
    )(w_mine, *args)[0]


def weight_parts(place, grad_half, att, att_other, early):
    feats, tokens = grad_half.shape
    shape = (2, 2, 2, feats // 8, HDIM)
    return kernel_call(
        weight_kernel, "weight_parts", [(shape, BF), (shape, F32)], [SM] + [VM] * 3 + [HB],
        [pltpu.VMEM((tokens, 2 * HDIM), BF), pltpu.VMEM((feats, 2 * HDIM), F32)],
        2_000_000_000,
    )(place, grad_half, att, att_other, early)


def shifted(block, distance):
    route = [(i - distance, i) for i in range(16) if 0 <= i - distance < 16]
    return lax.ppermute(block, ST, route)


def swapped(block):
    return lax.ppermute(block, "xl", [(0, 1), (1, 0)])


def halved(part, axis, distance, size, dim, bit):
    route = [(i, i ^ distance) for i in range(size)]
    send = lax.dynamic_index_in_dim(part, 1 - bit, dim, keepdims=False).astype(BF)
    keep = lax.dynamic_index_in_dim(part, bit, dim, keepdims=False)
    return keep, lax.ppermute(send, axis, route)


def body(queries, key_rows, value_rows, out_grad, proj_weight, pattern):
    half, y = lax.axis_index("xl"), lax.axis_index("y")
    tokens = queries.shape[1]
    place = jnp.stack((half, lax.axis_index("core"))).astype(jnp.int32)
    places = lax.axis_size("z")
    q = queries.reshape(BLOCK)
    keys, values = key_rows.reshape(BLOCK), value_rows.reshape(BLOCK)
    kv = jnp.stack((keys, values))
    above, below = shifted(kv, 1), shifted(kv, -1)

    block = out_grad[0].T
    feats = places * block.shape[0]
    copies = jnp.broadcast_to(block, (places,) + block.shape)
    grad_half = lax.all_to_all(copies, "z", 0, 0, tiled=True).reshape(feats, tokens)
    w_mine = lax.dynamic_slice_in_dim(proj_weight, half * feats, feats, 1)
    w_other = swapped(lax.dynamic_slice_in_dim(proj_weight, (1 - half) * feats, feats, 1))

    own_state = forward_own(pattern, q, keys, values)
    attended, att_flip, lse = forward_halo(pattern, q, *own_state, above, below, w_other)
    att = attended.reshape(tokens, HDIM)
    att_other = swapped(att)

    back_sent = dot(w_other, grad_half, NN).astype(BF)
    back_got = swapped(back_sent)
    back_mine = dot(w_mine, grad_half, NN)

    part = projected_part(w_mine, w_other, att, att_other, back_sent)
    parts = lax.all_to_all(part.reshape((places,) + block.shape), "z", 0, 0, tiled=True)
    projected = jnp.sum(parts.astype(F32), axis=0).astype(BF).T[None]

    sent, kept = weight_parts(place, grad_half, att, att_other, back_sent)
    got = lax.ppermute(sent, "core", [(0, 1), (1, 0)])
    kept, got = halved(kept + got.astype(F32), "xh", 1, 2, 2, lax.axis_index("xh"))

    up, down, dq_part, back, _ = backward_halo(
        pattern, q, back_mine, back_got, att_flip, lse, above, below, sent
    )
    up, down = shifted(up, -1), shifted(down, 1)
    dq, dk, dv, zero = backward_own(pattern, q, back, att_flip, lse, keys, values, dq_part, kept)

    kept = (kept + got.astype(F32) + zero).astype(BF).reshape((4,) + kept.shape[2:])
    summed = 0.0
    for k in range(4):
        piece = lax.dynamic_index_in_dim(kept, y ^ k, 0, keepdims=False)
        route = [
            (h * 4 + i, (i ^ k) // 2 * 4 + 2 * h + (i ^ k) % 2) for h in range(2) for i in range(4)
        ]
        summed = summed + lax.ppermute(piece, ("xl", "y"), route).astype(F32)
    weight_grad = summed.T

    shape = (1, tokens, HDIM)
    key_grad = SCALING * (dk + up[0].astype(F32) + down[0].astype(F32))
    value_grad = dv + up[1].astype(F32) + down[1].astype(F32)
    key_grad = key_grad.astype(BF).reshape(shape)
    value_grad = value_grad.astype(BF).reshape(shape)
    return projected, dq.reshape(shape), key_grad, value_grad, weight_grad


def solution(mesh):
    fine = Mesh(mesh.devices.reshape(2, 8, 4, 2, 2), ("xl", "z", "y", "xh", "core"))
    fsdp = ("xl", "z")
    rows = P(None, ST, fsdp)
    return jax.shard_map(
        body,
        mesh=fine,
        in_specs=(rows, rows, rows, rows, P(fsdp, None), P(ST, None)),
        out_specs=(rows, rows, rows, rows, P(fsdp, ST)),
        check_vma=False,
    )
```

profile of v0, /device:TPU:2, one launch (start us, length us, event | category | flops | bytes accessed | tf_op | source)
XLA Modules:
  0.0 137.5 jit_solution(17053431771640362146)
XLA Ops:
  0.6 2.6 %broadcast_in_dim.7 = bf16[8,96,1536]{2,1,0:T(8,128)(2,1)} broadcast(bf16[96,1536]{1,0:T(8,128)(2,1)} %bitcast.79), dimensions={1,2} | broadcast | bytes 2654208 | tf_op jit(solution)/shard_map/broadcast_in_dim | solution.py:341
  3.2 0.0 copy-start.1
  3.2 0.0 copy-start.2
  3.2 8.6 %all-to-all-start = ((bf16[8,96,1536]{2,1,0:T(8,128)(2,1)}), bf16[8,96,1536]{2,1,0:T(8,128)(2,1)S(1)}, u32[]{:S(2)}, u32[]{:S(2)}) async-start(bf16[8,96,1536]{2,1,0:T(8,128)(2,1)} %broadcast_in_dim.7), calls=%async_computation | async-start | bytes 4718592 | tf_op jit(solution)/shard_map/all_to_all | solution.py:342
  11.8 0.0 copy-start.8
  11.8 0.0 copy-done.1
  11.8 0.0 copy-done.2
  11.8 0.9 pad_maximum_fusion
  12.8 2.4 %collective-permute-start.1 = (bf16[2,4,384,128]{3,2,1,0:T(8,128)(2,1)}, bf16[2,4,384,128]{3,2,1,0:T(8,128)(2,1)}, u32[]{:S(2)}, u32[]{:S(2)}) collective-permute-start(bf16[2,4,384,128]{3,2,1,0:T(8,128)(2,1)} %pad_maximum_fusion), channel_id=1, source_target_pairs={{0,1},{1,2},{2,3},{3,4},{4,5},{5,6},{6,7},{7,8},{8,9},{9,10},{10,1... | collective-permute-start | bytes 2359304 | tf_op jit(solution)/shard_map/ppermute | solution.py:315
  15.2 1.3 collective-permute-start.2
  16.4 1.1 constant_dynamic-slice_fusion
  17.5 0.6 collective-permute-start
  18.1 0.0 copy-done.8
  18.1 1.0 copy-done.5
  19.1 4.1 %forward_own.1 = (f32[4,1,384]{2,1,0:T(1,128)S(1)}, f32[4,1,384]{2,1,0:T(1,128)S(1)}, f32[4,128,384]{2,1,0:T(8,128)S(1)}) custom-call(s32[4,27]{1,0:T(4,128)S(1)} %copy-done.8, bf16[4,384,128]{2,1,0:T(8,128)(2,1)S(1)} %bitcast.72, bf16[4,384,128]{2,1,0:T(8,128)(2,1)S(1)} %bitcast.66, bf16[4,384,128]{2,1,0:T(8,128)(2,1)S(1)} %bitcast.69), custom_call_target="tpu_custom_call" | custom-call | flops 3000000000 | bytes 4000000 | tf_op jit(solution)/shard_map/forward_own/pallas_call | solution.py:261
  23.2 2.2 %collective-permute-done.early_ref.other_ref = bf16[128,768]{1,0:T(8,128)(2,1)S(1)} collective-permute-done((bf16[128,768]{1,0:T(8,128)(2,1)S(1)}, bf16[128,768]{1,0:T(8,128)(2,1)S(1)}, u32[]{:S(2)}, u32[]{:S(2)}) %collective-permute-start) | collective-permute-done | bytes 196640 | tf_op jit(solution)/shard_map/ppermute | solution.py:319
  25.4 0.0 collective-permute-done.1.above_ref
  25.4 0.0 collective-permute-done.2.below_ref
  25.4 0.0 copy-done.6
  25.4 6.1 %forward_halo.1 = (bf16[4,384,128]{2,1,0:T(8,128)(2,1)}, bf16[4,128,384]{2,1,0:T(8,128)(2,1)S(1)}, f32[4,1,384]{2,1,0:T(1,128)S(1)}) custom-call(s32[4,27]{1,0:T(4,128)S(1)} %copy-done.8, bf16[4,384,128]{2,1,0:T(8,128)(2,1)S(1)} %bitcast.73, f32[4,1,384]{2,1,0:T(1,128)S(1)} %get-tuple-element.21.top_in, f32[4,1,384]{2,1,0:T(1,128)S(1)} %get-tuple-element.22.total_in, ...), custom_call_target="tpu_custom_call" | custom-call | flops 5000000000 | bytes 4000000 | tf_op jit(solution)/shard_map/forward_halo/pallas_call | solution.py:269
  31.5 0.0 copy-start.9
  31.5 0.7 copy-done.9
  32.3 0.5 collective-permute-start.3
  32.8 35.8 %all-to-all-done = bf16[8,96,1536]{2,1,0:T(8,128)(2,1)S(1)} async-done(((bf16[8,96,1536]{2,1,0:T(8,128)(2,1)}), bf16[8,96,1536]{2,1,0:T(8,128)(2,1)S(1)}, u32[]{:S(2)}, u32[]{:S(2)}) %all-to-all-start) | async-done | bytes 2359328 | tf_op jit(solution)/shard_map/all_to_all | solution.py:342
  68.6 0.5 convolution_convert_fusion.early_ref
  69.1 0.0 copy-start.3
  69.1 0.0 collective-permute-done.3.got_ref.other_ref
  69.2 2.3 %projected_part.1 = bf16[768,1536]{1,0:T(8,128)(2,1)S(1)} custom-call(bf16[128,768]{1,0:T(8,128)(2,1)S(1)} %get-tuple-element.40.mine_ref, bf16[128,768]{1,0:T(8,128)(2,1)S(1)} %collective-permute-done.early_ref.other_ref, bf16[1536,128]{1,0:T(8,128)(2,1)} %bitcast.5.att_ref, bf16[1536,128]{1,0:T(8,128)(2,1)} %collective-permute-done.3.got_ref.other_ref, ...), custom_call_target="tpu_custom_call" | custom-call | flops 2000000000 | bytes 4000000 | tf_op jit(solution)/shard_map/projected_part/pallas_call | solution.py:297
  71.5 0.0 copy-done.3
  71.5 0.0 copy-start
  71.5 1.4 %copy-done = bf16[768,1536]{1,0:T(8,128)(2,1)} copy-done((bf16[768,1536]{1,0:T(8,128)(2,1)}, bf16[768,1536]{1,0:T(8,128)(2,1)S(1)}, u32[]{:S(2)}) %copy-start) | copy-done | bytes 2359320
  72.9 4.4 %all-to-all-start.1 = ((bf16[8,96,1536]{2,1,0:T(8,128)(2,1)}), bf16[8,96,1536]{2,1,0:T(8,128)(2,1)}, u32[]{:S(2)}, u32[]{:S(2)}) async-start(bf16[8,96,1536]{2,1,0:T(8,128)(2,1)} %bitcast.64), calls=%async_computation.1 | async-start | bytes 4718592 | tf_op jit(solution)/shard_map/all_to_all | solution.py:356
  77.3 0.1 pad_add_fusion.place_ref
  77.4 0.6 collective-permute-start.4
  78.0 1.0 copy-done.4
  79.0 2.1 %weight_parts.1 = (bf16[2,2,2,96,128]{4,3,2,1,0:T(8,128)(2,1)S(1)}, f32[2,2,2,96,128]{4,3,2,1,0:T(8,128)S(1)}) custom-call(s32[2]{0:T(128)S(1)} %pad_add_fusion.place_ref, bf16[768,1536]{1,0:T(8,128)(2,1)S(1)} %bitcast.62, bf16[1536,128]{1,0:T(8,128)(2,1)} %bitcast.5.att_ref, bf16[1536,128]{1,0:T(8,128)(2,1)} %collective-permute-done.3.got_ref.other_ref, ...), custom_call_target="tpu_custom_call" | custom-call | flops 2000000000 | bytes 4000000 | tf_op jit(solution)/shard_map/weight_parts/pallas_call | solution.py:306
  81.2 0.0 copy-start.7
  81.2 0.0 copy-start.10
  81.2 0.1 collective-permute-start.5
  81.3 0.5 fusion.4.back_mine_ref
  81.8 0.9 collective-permute-done.5
  82.8 2.5 %collective-permute-start.8 = (bf16[2,2,96,128]{3,2,1,0:T(8,128)(2,1)S(1)}, bf16[2,2,96,128]{3,2,1,0:T(8,128)(2,1)S(1)}, u32[]{:S(2)}, u32[]{:S(2)}) collective-permute-start(bf16[2,2,96,128]{3,2,1,0:T(8,128)(2,1)S(1)} %fusion.3), channel_id=1, source_target_pairs={{0,2},{2,0},{1,3},{3,1},{4,6},{6,4},{5,7},{7,5},{8,10},{10,8},{9,1... | collective-permute-start | bytes 294920 | tf_op jit(solution)/shard_map/ppermute | solution.py:326
  85.3 4.2 %collective-permute-done.4.back_got_ref = bf16[128,1536]{1,0:T(8,128)(2,1)S(1)} collective-permute-done((bf16[128,1536]{1,0:T(8,128)(2,1)}, bf16[128,1536]{1,0:T(8,128)(2,1)S(1)}, u32[]{:S(2)}, u32[]{:S(2)}) %collective-permute-start.4) | collective-permute-done | bytes 393248 | tf_op jit(solution)/shard_map/ppermute | solution.py:319
  89.5 0.0 copy-done.7
  89.5 0.0 copy-done.10
  89.5 7.5 %backward_halo.1 = (bf16[2,4,384,128]{3,2,1,0:T(8,128)(2,1)S(1)}, bf16[2,4,384,128]{3,2,1,0:T(8,128)(2,1)S(1)}, f32[4,128,384]{2,1,0:T(8,128)S(1)}, bf16[4,128,384]{2,1,0:T(8,128)(2,1)S(1)}, f32[1,128]{1,0:T(1,128)}) custom-call(s32[4,27]{1,0:T(4,128)S(1)} %copy-done.8, bf16[4,384,128]{2,1,0:T(8,128)(2,1)S(1)} %bitcast.74, ...), custom_call_target="tpu_custom_call" | custom-call | flops 12000000000 | bytes 4000000 | tf_op jit(solution)/shard_map/backward_halo/pallas_call | solution.py:278
  97.0 1.3 collective-permute-start.6
  98.3 5.4 %collective-permute-start.7 = (bf16[2,4,384,128]{3,2,1,0:T(8,128)(2,1)S(1)}, bf16[2,4,384,128]{3,2,1,0:T(8,128)(2,1)S(1)}, u32[]{:S(2)}, u32[]{:S(2)}) collective-permute-start(bf16[2,4,384,128]{3,2,1,0:T(8,128)(2,1)S(1)} %get-tuple-element.34), channel_id=1, source_target_pairs={{0,1},{1,2},{2,3},{3,4},{4,5},{5,6},{6,7},{7,8},{8,9},{9,10},{10,1... | collective-permute-start | bytes 2359304 | tf_op jit(solution)/shard_map/ppermute | solution.py:315
  103.7 7.0 %backward_own.1 = (bf16[4,384,128]{2,1,0:T(8,128)(2,1)}, f32[4,384,128]{2,1,0:T(8,128)S(1)}, f32[4,384,128]{2,1,0:T(8,128)S(1)}, f32[1,128]{1,0:T(1,128)S(1)}) custom-call(s32[4,27]{1,0:T(4,128)S(1)} %copy-done.8, bf16[4,384,128]{2,1,0:T(8,128)(2,1)S(1)} %bitcast.75, bf16[4,128,384]{2,1,0:T(8,128)(2,1)S(1)} %get-tuple-element.28.back_ref, ...), custom_call_target="tpu_custom_call" | custom-call | flops 6000000000 | bytes 4000000 | tf_op jit(solution)/shard_map/backward_own/pallas_call | solution.py:288
  110.7 0.0 collective-permute-done.8
  110.8 5.7 %collective-permute-start.10 = (bf16[96,128]{1,0:T(8,128)(2,1)S(1)}, bf16[96,128]{1,0:T(8,128)(2,1)S(1)}, u32[]{:S(2)}, u32[]{:S(2)}) collective-permute-start(bf16[96,128]{1,0:T(8,128)(2,1)S(1)} %get-tuple-element.44), channel_id=1, source_target_pairs={{0,4},{4,0},{8,132},{12,128},{128,12},{132,8},{136,140},{140,136},... | collective-permute-start | bytes 73736 | tf_op jit(solution)/shard_map/ppermute | solution.py:376
  116.5 0.7 collective-permute-start.11
  117.2 0.0 collective-permute-start.12
  117.2 6.7 %collective-permute-done.10 = bf16[96,128]{1,0:T(8,128)(2,1)S(1)} collective-permute-done((bf16[96,128]{1,0:T(8,128)(2,1)S(1)}, bf16[96,128]{1,0:T(8,128)(2,1)S(1)}, u32[]{:S(2)}, u32[]{:S(2)}) %collective-permute-start.10) | collective-permute-done | bytes 24608 | tf_op jit(solution)/shard_map/ppermute | solution.py:376
  123.9 4.8 %collective-permute-start.9 = (bf16[96,128]{1,0:T(8,128)(2,1)S(1)}, bf16[96,128]{1,0:T(8,128)(2,1)S(1)}, u32[]{:S(2)}, u32[]{:S(2)}) collective-permute-start(bf16[96,128]{1,0:T(8,128)(2,1)S(1)} %get-tuple-element.41), channel_id=1, source_target_pairs={{0,0},{4,4},{8,128},{12,132},{128,8},{132,12},{136,136},{140,140},... | collective-permute-start | bytes 73736 | tf_op jit(solution)/shard_map/ppermute | solution.py:376
  128.7 0.0 collective-permute-done.11
  128.7 0.0 collective-permute-done.12
  128.7 3.3 %collective-permute-done.9 = bf16[96,128]{1,0:T(8,128)(2,1)S(1)} collective-permute-done((bf16[96,128]{1,0:T(8,128)(2,1)S(1)}, bf16[96,128]{1,0:T(8,128)(2,1)S(1)}, u32[]{:S(2)}, u32[]{:S(2)}) %collective-permute-start.9) | collective-permute-done | bytes 24608 | tf_op jit(solution)/shard_map/ppermute | solution.py:376
  132.0 0.6 add_bitcast_fusion
  132.6 0.0 collective-permute-done.6
  132.6 0.0 collective-permute-done.7
  132.6 1.2 fusion
  133.8 0.9 all-to-all-done.1
  134.7 2.8 %reduce_sum.12 = bf16[96,1536]{1,0:T(8,128)(2,1)} reduce(bf16[8,96,1536]{2,1,0:T(8,128)(2,1)} %all-to-all-done.1, bf16[]{:T(256)} %constant.43.clone.1), dimensions={0}, to_apply=%region_0.0 | reduce | flops 1032192 | bytes 2654210 | tf_op jit(solution)/shard_map/reduce_sum | solution.py:357
  (9 shorter events, 0.1 us)
Async XLA Ops:
  3.2 8.6 %copy-start.1 = (bf16[1,1536,128]{2,1,0:T(8,128)(2,1)S(1)}, bf16[1,1536,128]{2,1,0:T(8,128)(2,1)}, u32[]{:S(2)}) copy-start(bf16[1,1536,128]{2,1,0:T(8,128)(2,1)} %param.7) | copy-start | bytes 1179652
  3.2 8.6 %copy-start.2 = (bf16[1,1536,128]{2,1,0:T(8,128)(2,1)S(1)}, bf16[1,1536,128]{2,1,0:T(8,128)(2,1)}, u32[]{:S(2)}) copy-start(bf16[1,1536,128]{2,1,0:T(8,128)(2,1)} %param.8) | copy-start | bytes 1179652
  3.2 65.4 %all-to-all-start = ((bf16[8,96,1536]{2,1,0:T(8,128)(2,1)}), bf16[8,96,1536]{2,1,0:T(8,128)(2,1)S(1)}, u32[]{:S(2)}, u32[]{:S(2)}) async-start(bf16[8,96,1536]{2,1,0:T(8,128)(2,1)} %broadcast_in_dim.7), calls=%async_computation | async-start | bytes 4718592 | tf_op jit(solution)/shard_map/all_to_all | solution.py:342
  11.8 6.3 %copy-start.8 = (s32[4,27]{1,0:T(4,128)S(1)}, s32[4,27]{1,0:T(4,128)}, u32[]{:S(2)}) copy-start(s32[4,27]{1,0:T(4,128)} %pattern_ref.7) | copy-start | bytes 1300
  12.8 12.7 %collective-permute-start.1 = (bf16[2,4,384,128]{3,2,1,0:T(8,128)(2,1)}, bf16[2,4,384,128]{3,2,1,0:T(8,128)(2,1)}, u32[]{:S(2)}, u32[]{:S(2)}) collective-permute-start(bf16[2,4,384,128]{3,2,1,0:T(8,128)(2,1)} %pad_maximum_fusion), channel_id=1, source_target_pairs={{0,1},{1,2},{2,3},{3,4},{4,5},{5,6},{6,7},{7,8},{8,9},{9,10},{10,1... | collective-permute-start | bytes 2359304 | tf_op jit(solution)/shard_map/ppermute | solution.py:315
  15.2 10.3 %collective-permute-start.2 = (bf16[2,4,384,128]{3,2,1,0:T(8,128)(2,1)}, bf16[2,4,384,128]{3,2,1,0:T(8,128)(2,1)}, u32[]{:S(2)}, u32[]{:S(2)}) collective-permute-start(bf16[2,4,384,128]{3,2,1,0:T(8,128)(2,1)} %pad_maximum_fusion), channel_id=1, source_target_pairs={{1,0},{2,1},{3,2},{4,3},{5,4},{6,5},{7,6},{8,7},{9,8},{10,9},{11,1... | collective-permute-start | bytes 2359304 | tf_op jit(solution)/shard_map/ppermute | solution.py:315
  17.5 7.9 %collective-permute-start = (bf16[128,768]{1,0:T(8,128)(2,1)S(1)}, bf16[128,768]{1,0:T(8,128)(2,1)S(1)}, u32[]{:S(2)}, u32[]{:S(2)}) collective-permute-start(bf16[128,768]{1,0:T(8,128)(2,1)S(1)} %get-tuple-element.39), channel_id=1, source_target_pairs={{0,128},{128,0},{1,129},{129,1},{2,130},{130,2},{3,131},{131,3},{4... | collective-permute-start | bytes 589832 | tf_op jit(solution)/shard_map/ppermute | solution.py:319
  18.1 1.0 copy-start.5
  19.1 6.3 %copy-start.6 = (bf16[1,1536,128]{2,1,0:T(8,128)(2,1)S(1)}, bf16[1,1536,128]{2,1,0:T(8,128)(2,1)}, u32[]{:S(2)}) copy-start(bf16[1,1536,128]{2,1,0:T(8,128)(2,1)} %param.6) | copy-start | bytes 1179652
  31.5 0.7 copy-start.9
  32.3 36.9 %collective-permute-start.3 = (bf16[1536,128]{1,0:T(8,128)(2,1)}, bf16[1536,128]{1,0:T(8,128)(2,1)}, u32[]{:S(2)}, u32[]{:S(2)}) collective-permute-start(bf16[1536,128]{1,0:T(8,128)(2,1)} %bitcast.5.att_ref), channel_id=1, source_target_pairs={{0,128},{128,0},{1,129},{129,1},{2,130},{130,2},{3,131},{131,3},{4... | collective-permute-start | bytes 1179656 | tf_op jit(solution)/shard_map/ppermute | solution.py:319
  69.1 2.4 %copy-start.3 = (bf16[128,1536]{1,0:T(8,128)(2,1)}, bf16[128,1536]{1,0:T(8,128)(2,1)S(1)}, u32[]{:S(2)}) copy-start(bf16[128,1536]{1,0:T(8,128)(2,1)S(1)} %convolution_convert_fusion.early_ref) | copy-start | bytes 1179652
  71.5 1.4 %copy-start = (bf16[768,1536]{1,0:T(8,128)(2,1)}, bf16[768,1536]{1,0:T(8,128)(2,1)S(1)}, u32[]{:S(2)}) copy-start(bf16[768,1536]{1,0:T(8,128)(2,1)S(1)} %projected_part.1) | copy-start | bytes 7077892
  72.9 61.7 %all-to-all-start.1 = ((bf16[8,96,1536]{2,1,0:T(8,128)(2,1)}), bf16[8,96,1536]{2,1,0:T(8,128)(2,1)}, u32[]{:S(2)}, u32[]{:S(2)}) async-start(bf16[8,96,1536]{2,1,0:T(8,128)(2,1)} %bitcast.64), calls=%async_computation.1 | async-start | bytes 4718592 | tf_op jit(solution)/shard_map/all_to_all | solution.py:356
  77.4 12.1 %collective-permute-start.4 = (bf16[128,1536]{1,0:T(8,128)(2,1)}, bf16[128,1536]{1,0:T(8,128)(2,1)S(1)}, u32[]{:S(2)}, u32[]{:S(2)}) collective-permute-start(bf16[128,1536]{1,0:T(8,128)(2,1)} %copy-done.3), channel_id=1, source_target_pairs={{0,128},{128,0},{1,129},{129,1},{2,130},{130,2},{3,131},{131,3},{4... | collective-permute-start | bytes 1179656 | tf_op jit(solution)/shard_map/ppermute | solution.py:319
  78.0 1.0 copy-start.4
  81.2 8.3 %copy-start.7 = (bf16[1,1536,128]{2,1,0:T(8,128)(2,1)S(1)}, bf16[1,1536,128]{2,1,0:T(8,128)(2,1)}, u32[]{:S(2)}) copy-start(bf16[1,1536,128]{2,1,0:T(8,128)(2,1)} %param.6) | copy-start | bytes 1179652
  81.2 8.3 %copy-start.10 = (bf16[4,128,384]{2,1,0:T(8,128)(2,1)S(1)}, bf16[4,128,384]{2,1,0:T(8,128)(2,1)}, u32[]{:S(2)}) copy-start(bf16[4,128,384]{2,1,0:T(8,128)(2,1)} %copy-done.9) | copy-start | bytes 1179652
  81.2 1.5 %collective-permute-start.5 = (bf16[2,2,2,96,128]{4,3,1,0,2:T(8,128)(2,1)S(1)}, bf16[2,2,2,96,128]{4,3,1,0,2:T(8,128)(2,1)S(1)}, u32[]{:S(2)}, u32[]{:S(2)}) collective-permute-start(bf16[2,2,2,96,128]{4,3,1,0,2:T(8,128)(2,1)S(1)} %copy.11), channel_id=1, source_target_pairs={{0,1},{1,0},{2,3},{3,2},{4,5},{5,4},{6,7},{7,6},{8,9},{9,8},{10,11... | collective-permute-start | bytes 589832 | tf_op jit(solution)/shard_map/ppermute | solution.py:360
  82.8 27.9 %collective-permute-start.8 = (bf16[2,2,96,128]{3,2,1,0:T(8,128)(2,1)S(1)}, bf16[2,2,96,128]{3,2,1,0:T(8,128)(2,1)S(1)}, u32[]{:S(2)}, u32[]{:S(2)}) collective-permute-start(bf16[2,2,96,128]{3,2,1,0:T(8,128)(2,1)S(1)} %fusion.3), channel_id=1, source_target_pairs={{0,2},{2,0},{1,3},{3,1},{4,6},{6,4},{5,7},{7,5},{8,10},{10,8},{9,1... | collective-permute-start | bytes 294920 | tf_op jit(solution)/shard_map/ppermute | solution.py:326
  97.0 35.6 %collective-permute-start.6 = (bf16[2,4,384,128]{3,2,1,0:T(8,128)(2,1)S(1)}, bf16[2,4,384,128]{3,2,1,0:T(8,128)(2,1)S(1)}, u32[]{:S(2)}, u32[]{:S(2)}) collective-permute-start(bf16[2,4,384,128]{3,2,1,0:T(8,128)(2,1)S(1)} %get-tuple-element.33), channel_id=1, source_target_pairs={{1,0},{2,1},{3,2},{4,3},{5,4},{6,5},{7,6},{8,7},{9,8},{10,9},{11,1... | collective-permute-start | bytes 2359304 | tf_op jit(solution)/shard_map/ppermute | solution.py:315
  98.3 34.3 %collective-permute-start.7 = (bf16[2,4,384,128]{3,2,1,0:T(8,128)(2,1)S(1)}, bf16[2,4,384,128]{3,2,1,0:T(8,128)(2,1)S(1)}, u32[]{:S(2)}, u32[]{:S(2)}) collective-permute-start(bf16[2,4,384,128]{3,2,1,0:T(8,128)(2,1)S(1)} %get-tuple-element.34), channel_id=1, source_target_pairs={{0,1},{1,2},{2,3},{3,4},{4,5},{5,6},{6,7},{7,8},{8,9},{9,10},{10,1... | collective-permute-start | bytes 2359304 | tf_op jit(solution)/shard_map/ppermute | solution.py:315
  110.8 13.1 %collective-permute-start.10 = (bf16[96,128]{1,0:T(8,128)(2,1)S(1)}, bf16[96,128]{1,0:T(8,128)(2,1)S(1)}, u32[]{:S(2)}, u32[]{:S(2)}) collective-permute-start(bf16[96,128]{1,0:T(8,128)(2,1)S(1)} %get-tuple-element.44), channel_id=1, source_target_pairs={{0,4},{4,0},{8,132},{12,128},{128,12},{132,8},{136,140},{140,136},... | collective-permute-start | bytes 73736 | tf_op jit(solution)/shard_map/ppermute | solution.py:376
  116.5 12.2 %collective-permute-start.11 = (bf16[96,128]{1,0:T(8,128)(2,1)S(1)}, bf16[96,128]{1,0:T(8,128)(2,1)S(1)}, u32[]{:S(2)}, u32[]{:S(2)}) collective-permute-start(bf16[96,128]{1,0:T(8,128)(2,1)S(1)} %get-tuple-element.43), channel_id=1, source_target_pairs={{0,128},{4,132},{8,0},{12,4},{128,136},{132,140},{136,8},{140,12},... | collective-permute-start | bytes 73736 | tf_op jit(solution)/shard_map/ppermute | solution.py:376
  117.2 11.5 %collective-permute-start.12 = (bf16[96,128]{1,0:T(8,128)(2,1)S(1)}, bf16[96,128]{1,0:T(8,128)(2,1)S(1)}, u32[]{:S(2)}, u32[]{:S(2)}) collective-permute-start(bf16[96,128]{1,0:T(8,128)(2,1)S(1)} %get-tuple-element.42), channel_id=1, source_target_pairs={{0,132},{4,128},{8,4},{12,0},{128,140},{132,136},{136,12},{140,8},... | collective-permute-start | bytes 73736 | tf_op jit(solution)/shard_map/ppermute | solution.py:376
  123.9 8.1 %collective-permute-start.9 = (bf16[96,128]{1,0:T(8,128)(2,1)S(1)}, bf16[96,128]{1,0:T(8,128)(2,1)S(1)}, u32[]{:S(2)}, u32[]{:S(2)}) collective-permute-start(bf16[96,128]{1,0:T(8,128)(2,1)S(1)} %get-tuple-element.41), channel_id=1, source_target_pairs={{0,0},{4,4},{8,128},{12,132},{128,8},{132,12},{136,136},{140,140},... | collective-permute-start | bytes 73736 | tf_op jit(solution)/shard_map/ppermute | solution.py:376
where the time goes:
time: 140 us; the launch traced here: 137 us
  waiting for transfers between devices  54 us (39%)
  starting transfers between devices  38.8 us (28%)
  Pallas kernels  29.1 us (21%)
  local copies, waits for them, and re-layouts  7.93 us (6%)
  other arithmetic  5.67 us (4%)
    all_to_all x1, waiting for transfers between devices, body(): lax.all_to_all(copies, 'z', 0, 0, tiled=True).reshape(feats, tokens)  35.8 us
    ppermute x4, starting transfers between devices, body(): summed = summed + lax.ppermute(piece, ('xl', 'y'), route).astype(F32)  11.3 us
    ppermute x4, starting transfers between devices, shifted(): return lax.ppermute(block, ST, route)  10.3 us
    ppermute x4, waiting for transfers between devices, body(): summed = summed + lax.ppermute(piece, ('xl', 'y'), route).astype(F32)  9.92 us
    all_to_all x1, starting transfers between devices, body(): lax.all_to_all(copies, 'z', 0, 0, tiled=True).reshape(feats, tokens)  8.6 us
    pallas_call x1, Pallas kernels, backward_halo(): kernel_call(backward_halo_kernel, 'backward_halo', outs, [SM] + [VM] * 5...  7.52 us
    pallas_call x1, Pallas kernels, backward_own(): kernel_call(backward_own_kernel, 'backward_own', outs, [SM] + [VM] * 7 +...  7.03 us
    ppermute x3, waiting for transfers between devices, swapped(): return lax.ppermute(block, 'xl', [(0, 1), (1, 0)])  6.41 us
  transfers between devices with their start and end apart: 15, of which 7 were waited for; matrix products, arithmetic and copies ran while one was open for 4% of the time, Pallas kernels for 20%

commit v1 on v0

--- a/solution.py
+++ b/solution.py
@@ -96,7 +96,8 @@
 
 
 def forward_own_kernel(
-    pattern_ref, q_ref, k_ref, v_ref, top, total, acc, tile_of, place_of, s0, s1, m0, m1
+    pattern_ref, q_ref, k_ref, v_ref, e0, e1,
+    top, total, acc, tile_of, place_of, s0, s1, m0, m1,
 ):
     count = build_pairs(pattern_ref, tile_of, place_of, (1,))
     top[...] = jnp.full(top.shape, -jnp.inf, F32)
@@ -156,7 +157,6 @@
 
 def backward_halo_kernel(
     pattern_ref, q_ref, back_mine_ref, back_got_ref, att_ref, lse_ref, above_ref, below_ref,
-    early_ref,
     up_ref, down_ref, dq, back_ref, zero_ref,
     kband, vband, tile_of, place_of, p0, p1, d0, d1, delta, dk, dv, sem,
 ):
@@ -183,13 +183,13 @@
 
 
 def backward_own_kernel(
-    pattern_ref, q_ref, back_ref, att_ref, lse_ref, k_ref, v_ref, dq_in, early_ref,
-    dq_ref, dk, dv, zero_ref,
-    tile_of, place_of, p0, p1, d0, d1, delta, dq,
+    pattern_ref, q_ref, back_ref, att_ref, lse_ref, k_ref, v_ref, dq_in, up_ref, down_ref,
+    dq_ref, dk_ref, dv_ref, zero_ref,
+    tile_of, place_of, p0, p1, d0, d1, delta, dq, dk, dv,
 ):
     count = build_pairs(pattern_ref, tile_of, place_of, (1,))
-    dk[...] = jnp.zeros(dk.shape, F32)
-    dv[...] = jnp.zeros(dv.shape, F32)
+    dk[...] = up_ref[0].astype(F32) + down_ref[0].astype(F32)
+    dv[...] = up_ref[1].astype(F32) + down_ref[1].astype(F32)
     zero_ref[...] = jnp.zeros(zero_ref.shape, F32)
     dq[...] = dq_in[...]
     backward_pairs(
@@ -198,9 +198,29 @@
     )
     for tile in range(ROW_TILES):
         dq_ref[tile] = (dq[tile] * SCALING).T.astype(BF)
-
-
-def part_kernel(mine_ref, other_ref, att_ref, got_ref, early_ref, part_ref, weights, heads):
+        dk_ref[tile] = (dk[tile] * SCALING).astype(BF)
+        dv_ref[tile] = dv[tile].astype(BF)
+
+
+def back_kernel(place_ref, other_ref, mine_ref, *refs):
+    blocks, (grad, sent_ref, kept_ref) = refs[:-3], refs[-3:]
+    rows, tokens = blocks[0].shape
+
+    def at(offset):
+        source = lax.rem(place_ref[2] + offset + 8, 8)
+        return pl.ds(pl.multiple_of(source * rows, 32), rows)
+
+    for offset, block in zip(RING, blocks):
+        grad[at(offset)] = block[...]
+    grad[at(4), : tokens // 2] = blocks[-2][...]
+    grad[at(4), tokens // 2 :] = blocks[-1][...]
+    sent_ref[...] = dot(other_ref[...], grad[...], NN).astype(BF)
+    kept_ref[...] = dot(mine_ref[...], grad[...], NN)
+
+
+def part_kernel(place_ref, mine_ref, other_ref, att_ref, got_ref, early_ref, *refs):
+    blocks, (weights, heads, total) = refs[:-3], refs[-3:]
+    rows, tokens = blocks[0].shape
     weights[:HDIM] = mine_ref[...]
     weights[HDIM:] = other_ref[...]
     heads[:, :HDIM] = att_ref[...]
@@ -208,7 +228,16 @@
     for tile in range(ROW_TILES):
         cols = slice(tile * TILE, (tile + 1) * TILE)
         terms = dot(weights[...], heads[cols], (((0,), (1,)), ((), ())))
-        part_ref[:, cols] = terms.astype(BF)
+        total[:, cols] = terms.astype(BF)
+
+    def at(offset):
+        target = lax.rem(place_ref[2] + offset + 8, 8)
+        return pl.ds(pl.multiple_of(target * rows, 32), rows)
+
+    for offset, block in zip(RING, blocks):
+        block[...] = total[at(offset)]
+    blocks[-2][...] = total[at(4), : tokens // 2]
+    blocks[-1][...] = total[at(4), tokens // 2 :]
 
 
 def weight_kernel(place_ref, grad_ref, att_ref, other_ref, early_ref, send_ref, keep_ref, heads, total):
@@ -231,9 +260,11 @@
 VM = pl.BlockSpec(memory_space=pltpu.VMEM)
 SM = pl.BlockSpec(memory_space=pltpu.SMEM)
 HB = pl.BlockSpec(memory_space=pltpu.HBM)
+ANY = pl.BlockSpec(memory_space=pl.ANY)
 BLOCK = (ROW_TILES, TILE, HDIM)
 FLIP = (ROW_TILES, HDIM, TILE)
 LINE = (ROW_TILES, 1, TILE)
+RING = (0, -1, 1, -2, 2, -3, 3)
 HALO = (2 * ROW_TILES, TILE, HDIM)
 PAIR_LISTS = [pltpu.SMEM((49,), jnp.int32), pltpu.SMEM((49,), jnp.int32)]
 HALO_BAND = [pltpu.VMEM(HALO, BF), pltpu.VMEM(HALO, BF)]
@@ -260,7 +291,7 @@
 def forward_own(*args):
     return kernel_call(
         forward_own_kernel, "forward_own", [(LINE, F32), (LINE, F32), (FLIP, F32)],
-        [SM, VM, VM, VM], PAIR_LISTS + SCORES, 3_000_000_000,
+        [SM, VM, VM, VM, ANY, ANY], PAIR_LISTS + SCORES, 3_000_000_000,
     )(*args)
 
 
@@ -268,7 +299,7 @@
     state = [pltpu.VMEM(LINE, F32), pltpu.VMEM(LINE, F32), pltpu.VMEM(FLIP, F32)]
     return kernel_call(
         forward_halo_kernel, "forward_halo", [(BLOCK, BF), (FLIP, BF), (LINE, F32)],
-        [SM] + [VM] * 4 + [HB] * 3, HALO_BAND + PAIR_LISTS + SCORES + state + [DMA_SEMS],
+        [SM] + [VM] * 4 + [HB] * 2 + [ANY], HALO_BAND + PAIR_LISTS + SCORES + state + [DMA_SEMS],
         5_000_000_000,
     )(*args)
 
@@ -276,7 +307,7 @@
 def backward_halo(*args):
     outs = [((2,) + BLOCK, BF), ((2,) + BLOCK, BF), (FLIP, F32), (FLIP, BF), ((1, HDIM), F32)]
     return kernel_call(
-        backward_halo_kernel, "backward_halo", outs, [SM] + [VM] * 5 + [HB] * 3,
+        backward_halo_kernel, "backward_halo", outs, [SM] + [VM] * 5 + [HB] * 2,
         HALO_BAND + PAIR_LISTS + TERMS
         + [pltpu.VMEM(LINE, F32), pltpu.VMEM(HALO, F32), pltpu.VMEM(HALO, F32), DMA_SEMS],
         12_000_000_000,
@@ -284,20 +315,36 @@
 
 
 def backward_own(*args):
-    outs = [(BLOCK, BF), (BLOCK, F32), (BLOCK, F32), ((1, HDIM), F32)]
-    return kernel_call(
-        backward_own_kernel, "backward_own", outs, [SM] + [VM] * 7 + [HB],
-        PAIR_LISTS + TERMS + [pltpu.VMEM(LINE, F32), pltpu.VMEM(FLIP, F32)],
+    outs = [(BLOCK, BF), (BLOCK, BF), (BLOCK, BF), ((1, HDIM), F32)]
+    return kernel_call(
+        backward_own_kernel, "backward_own", outs, [SM] + [VM] * 9,
+        PAIR_LISTS + TERMS
+        + [pltpu.VMEM(LINE, F32), pltpu.VMEM(FLIP, F32)] + [pltpu.VMEM(BLOCK, F32)] * 2,
         6_000_000_000,
     )(*args)
 
 
-def projected_part(w_mine, *args):
+def back_parts(place, w_other, w_mine, blocks):
+    heads, feats = w_mine.shape
+    tokens = blocks[0].shape[1]
+    outs = [((feats, tokens), BF), ((heads, tokens), BF), ((heads, tokens), F32)]
+    return kernel_call(
+        back_kernel, "back_parts", outs, [SM] + [VM] * (2 + len(blocks)), [], 2_000_000_000
+    )(place, w_other, w_mine, *blocks)
+
+
+def projected_parts(place, w_mine, *args):
     feats, tokens = w_mine.shape[1], ROW_TILES * TILE
-    return kernel_call(
-        part_kernel, "projected_part", [((feats, tokens), BF)], [VM] * 4 + [HB],
-        [pltpu.VMEM((2 * HDIM, feats), BF), pltpu.VMEM((tokens, 2 * HDIM), BF)], 2_000_000_000,
-    )(w_mine, *args)[0]
+    outs = [((feats // 8, tokens), BF)] * 7 + [((feats // 8, tokens // 2), BF)] * 2
+    return kernel_call(
+        part_kernel, "projected_parts", outs, [SM] + [VM] * 4 + [ANY],
+        [
+            pltpu.VMEM((2 * HDIM, feats), BF),
+            pltpu.VMEM((tokens, 2 * HDIM), BF),
+            pltpu.VMEM((feats, tokens), BF),
+        ],
+        2_000_000_000,
+    )(place, w_mine, *args)
 
 
 def weight_parts(place, grad_half, att, att_other, early):
@@ -326,10 +373,45 @@
     return keep, lax.ppermute(send, axis, route)
 
 
+def ring_gathered(block):
+    size = lax.axis_size("z")
+    onward = [(i, (i + 1) % size) for i in range(size)]
+    backward = [(j, i) for i, j in onward]
+    right = left = block
+    got = [block]
+    for _ in range(size // 2 - 1):
+        right, left = lax.ppermute(right, "z", onward), lax.ppermute(left, "z", backward)
+        got += [right, left]
+    middle = block.shape[1] // 2
+    far = [lax.ppermute(right[:, :middle], "z", onward), lax.ppermute(left[:, middle:], "z", backward)]
+    return got + far
+
+
+def ring_summed(parts, late):
+    size = lax.axis_size("z")
+    onward = [(i, (i + 1) % size) for i in range(size)]
+    backward = [(j, i) for i, j in onward]
+    middle = parts[-1].shape[1]
+    right = lax.ppermute(parts[-2], "z", onward).astype(F32)
+    left = lax.ppermute(parts[-1], "z", backward).astype(F32)
+    by_offset = {offset: part.astype(F32) for offset, part in zip(RING, parts)}
+    last = size // 2 - 1
+    right = jnp.concatenate((by_offset[last][:, :middle] + right, by_offset[last][:, middle:]), axis=1)
+    left = jnp.concatenate((by_offset[-last][:, :middle], by_offset[-last][:, middle:] + left), axis=1)
+    for offset in range(last - 1, -1, -1):
+        if offset == 0:
+            right, left = right + late, left + late
+        right = lax.ppermute(right.astype(BF), "z", onward).astype(F32)
+        left = lax.ppermute(left.astype(BF), "z", backward).astype(F32)
+        if offset:
+            right, left = right + by_offset[offset], left + by_offset[-offset]
+    return right + left + by_offset[0]
+
+
 def body(queries, key_rows, value_rows, out_grad, proj_weight, pattern):
     half, y = lax.axis_index("xl"), lax.axis_index("y")
     tokens = queries.shape[1]
-    place = jnp.stack((half, lax.axis_index("core"))).astype(jnp.int32)
+    place = jnp.stack((half, lax.axis_index("core"), lax.axis_index("z"))).astype(jnp.int32)
     places = lax.axis_size("z")
     q = queries.reshape(BLOCK)
     keys, values = key_rows.reshape(BLOCK), value_rows.reshape(BLOCK)
@@ -338,35 +420,34 @@
 
     block = out_grad[0].T
     feats = places * block.shape[0]
-    copies = jnp.broadcast_to(block, (places,) + block.shape)
-    grad_half = lax.all_to_all(copies, "z", 0, 0, tiled=True).reshape(feats, tokens)
+    blocks = ring_gathered(block)
     w_mine = lax.dynamic_slice_in_dim(proj_weight, half * feats, feats, 1)
     w_other = swapped(lax.dynamic_slice_in_dim(proj_weight, (1 - half) * feats, feats, 1))
 
-    own_state = forward_own(pattern, q, keys, values)
-    attended, att_flip, lse = forward_halo(pattern, q, *own_state, above, below, w_other)
+    grad_half, back_sent, back_mine = back_parts(place, w_other, w_mine, blocks)
+    back_got = swapped(back_sent)
+
+    own_state = forward_own(pattern, q, keys, values, above, below)
+    attended, att_flip, lse = forward_halo(pattern, q, *own_state, above, below, back_sent)
     att = attended.reshape(tokens, HDIM)
     att_other = swapped(att)
 
-    back_sent = dot(w_other, grad_half, NN).astype(BF)
-    back_got = swapped(back_sent)
-    back_mine = dot(w_mine, grad_half, NN)
-
-    part = projected_part(w_mine, w_other, att, att_other, back_sent)
-    parts = lax.all_to_all(part.reshape((places,) + block.shape), "z", 0, 0, tiled=True)
-    projected = jnp.sum(parts.astype(F32), axis=0).astype(BF).T[None]
-
-    sent, kept = weight_parts(place, grad_half, att, att_other, back_sent)
+    up, down, dq_part, back, zero = backward_halo(
+        pattern, q, back_mine, back_got, att_flip, lse, above, below
+    )
+    up, down = shifted(up, -1), shifted(down, 1)
+    dq, dk, dv, late = backward_own(
+        pattern, q, back, att_flip, lse, keys, values, dq_part, up, down
+    )
+
+    parts = projected_parts(place, w_mine, w_other, att, att_other, zero)
+    projected = ring_summed(parts, late[:, :1]).astype(BF).T[None]
+
+    sent, kept = weight_parts(place, grad_half, att, att_other, zero)
     got = lax.ppermute(sent, "core", [(0, 1), (1, 0)])
     kept, got = halved(kept + got.astype(F32), "xh", 1, 2, 2, lax.axis_index("xh"))
 
-    up, down, dq_part, back, _ = backward_halo(
-        pattern, q, back_mine, back_got, att_flip, lse, above, below, sent
-    )
-    up, down = shifted(up, -1), shifted(down, 1)
-    dq, dk, dv, zero = backward_own(pattern, q, back, att_flip, lse, keys, values, dq_part, kept)
-
-    kept = (kept + got.astype(F32) + zero).astype(BF).reshape((4,) + kept.shape[2:])
+    kept = (kept + got.astype(F32)).astype(BF).reshape((4,) + kept.shape[2:])
     summed = 0.0
     for k in range(4):
         piece = lax.dynamic_index_in_dim(kept, y ^ k, 0, keepdims=False)
@@ -377,11 +458,7 @@
     weight_grad = summed.T
 
     shape = (1, tokens, HDIM)
-    key_grad = SCALING * (dk + up[0].astype(F32) + down[0].astype(F32))
-    value_grad = dv + up[1].astype(F32) + down[1].astype(F32)
-    key_grad = key_grad.astype(BF).reshape(shape)
-    value_grad = value_grad.astype(BF).reshape(shape)
-    return projected, dq.reshape(shape), key_grad, value_grad, weight_grad
+    return projected, dq.reshape(shape), dk.reshape(shape), dv.reshape(shape), weight_grad
 
 
 def solution(mesh):

time: 140 us -> 128 us (0.914)
  waiting for transfers between devices: 54 us -> 30 us
  starting transfers between devices: 38.8 us -> 61.3 us
  local copies, waits for them, and re-layouts: 7.93 us -> 3.26 us
  Pallas kernels: 29.1 us -> 26.8 us
  other arithmetic: 5.67 us -> 4.2 us
    all_to_all x2 -> x0, waiting for transfers between devices: 36.7 us -> none  [the longest x1 35.8 us: body(): lax.all_to_all(copies, 'z', 0, 0, tiled=True).reshape(feats, tokens)]
    ppermute x0 -> x16, starting transfers between devices: none -> 31.6 us  [the longest x3 13.3 us: ring_gathered(): lax.ppermute(left, 'z', backward)]
    ppermute x0 -> x16, waiting for transfers between devices: none -> 19.9 us  [the longest x3 11.4 us: ring_gathered(): lax.ppermute(left, 'z', backward)]
    all_to_all x2 -> x0, starting transfers between devices: 13 us -> none  [the longest x1 8.6 us: body(): lax.all_to_all(copies, 'z', 0, 0, tiled=True).reshape(feats, tokens)]
    ppermute x4, waiting for transfers between devices: 9.92 us -> 3.32 us  [body(): summed = summed + lax.ppermute(piece, ('xl', 'y'), route).astype(F32)]
    ppermute x1, waiting for transfers between devices: 0.01 us -> 3.78 us  [halved(): return (keep, lax.ppermute(send, axis, route))]
    ppermute x3, waiting for transfers between devices: 6.41 us -> 3.01 us  [swapped(): return lax.ppermute(block, 'xl', [(0, 1), (1, 0)])]
    ppermute x4, starting transfers between devices: 10.3 us -> 7.16 us  [shifted(): return lax.ppermute(block, ST, route)]
  transfers between devices with their start and end apart: 15 -> 29, of which waited for: 7 -> 14; matrix products, arithmetic and copies ran while one was open for 4% -> 4% of each run, Pallas kernels for 20% -> 18%
where the time goes in v1:
time: 128 us; the launch traced here: 127 us
  starting transfers between devices  61.3 us (48%)
  waiting for transfers between devices  30 us (23%)
  Pallas kernels  26.8 us (21%)
  other arithmetic  4.2 us (3%)
  local copies, waits for them, and re-layouts  3.26 us (3%)
    ppermute x4, starting transfers between devices, body(): summed = summed + lax.ppermute(piece, ('xl', 'y'), route).astype(F32)  14.4 us
    ppermute x3, starting transfers between devices, ring_gathered(): lax.ppermute(left, 'z', backward)  13.3 us
    ppermute x3, waiting for transfers between devices, ring_gathered(): lax.ppermute(left, 'z', backward)  11.4 us
    ppermute x3, starting transfers between devices, ring_summed(): left = lax.ppermute(left.astype(BF), 'z', backward).astype(F32)  10.8 us
    ppermute x4, starting transfers between devices, shifted(): return lax.ppermute(block, ST, route)  7.16 us
    pallas_call x1, Pallas kernels, backward_halo(): kernel_call(backward_halo_kernel, 'backward_halo', outs, [SM] + [VM] * 5...  6.72 us
    pallas_call x1, Pallas kernels, backward_own(): kernel_call(backward_own_kernel, 'backward_own', outs, [SM] + [VM] * 9, P...  6.24 us
    pallas_call x1, Pallas kernels, forward_halo(): kernel_call(forward_halo_kernel, 'forward_halo', [(BLOCK, BF), (FLIP, BF)...  4.82 us
  transfers between devices with their start and end apart: 29, of which 14 were waited for; matrix products, arithmetic and copies ran while one was open for 4% of the time, Pallas kernels for 18%

profile of v1, /device:TPU:2, one launch (start us, length us, event | category | flops | bytes accessed | tf_op | source)
XLA Modules:
  0.0 126.6 jit_solution(11419921660538891984)
XLA Ops:
  0.7 5.9 %collective-permute-start.4 = (bf16[96,1536]{1,0:T(8,128)(2,1)}, bf16[96,1536]{1,0:T(8,128)(2,1)S(1)}, u32[]{:S(2)}, u32[]{:S(2)}) collective-permute-start(bf16[96,1536]{1,0:T(8,128)(2,1)} %bitcast.53), channel_id=1, source_target_pairs={{16,0},{32,16},{48,32},{64,48},{80,64},{96,80},{112,96},{0,112},{1... | collective-permute-start | bytes 884744 | tf_op jit(solution)/shard_map/ppermute | solution.py:383
  6.6 0.0 collective-permute-start.3
  6.6 2.1 %pad_maximum_fusion = bf16[2,4,384,128]{3,2,1,0:T(8,128)(2,1)} fusion(bf16[1,4,384,128]{3,2,1,0:T(8,128)(2,1)} %bitcast.41, bf16[1,4,384,128]{3,2,1,0:T(8,128)(2,1)} %bitcast.38), kind=kLoop, calls=%fused_computation | loop fusion | flops 393216 | bytes 1572864 | tf_op jit(solution)/shard_map/stack | solution.py:418
  8.7 1.5 %collective-permute-start.1 = (bf16[2,4,384,128]{3,2,1,0:T(8,128)(2,1)}, bf16[2,4,384,128]{3,2,1,0:T(8,128)(2,1)S(1)}, u32[]{:S(2)}, u32[]{:S(2)}) collective-permute-start(bf16[2,4,384,128]{3,2,1,0:T(8,128)(2,1)} %pad_maximum_fusion), channel_id=1, source_target_pairs={{0,1},{1,2},{2,3},{3,4},{4,5},{5,6},{6,7},{7,8},{8,9},{9,10},{10,1... | collective-permute-start | bytes 2359304 | tf_op jit(solution)/shard_map/ppermute | solution.py:362
  10.2 1.3 %collective-permute-start.2 = (bf16[2,4,384,128]{3,2,1,0:T(8,128)(2,1)}, bf16[2,4,384,128]{3,2,1,0:T(8,128)(2,1)S(1)}, u32[]{:S(2)}, u32[]{:S(2)}) collective-permute-start(bf16[2,4,384,128]{3,2,1,0:T(8,128)(2,1)} %pad_maximum_fusion), channel_id=1, source_target_pairs={{1,0},{2,1},{3,2},{4,3},{5,4},{6,5},{7,6},{8,7},{9,8},{10,9},{11,1... | collective-permute-start | bytes 2359304 | tf_op jit(solution)/shard_map/ppermute | solution.py:362
  11.5 1.7 %collective-permute-done.4.refs_2_ = bf16[96,1536]{1,0:T(8,128)(2,1)S(1)} collective-permute-done((bf16[96,1536]{1,0:T(8,128)(2,1)}, bf16[96,1536]{1,0:T(8,128)(2,1)S(1)}, u32[]{:S(2)}, u32[]{:S(2)}) %collective-permute-start.4) | collective-permute-done | bytes 294944 | tf_op jit(solution)/shard_map/ppermute | solution.py:383
  13.2 3.6 %collective-permute-start.6 = (bf16[96,1536]{1,0:T(8,128)(2,1)S(1)}, bf16[96,1536]{1,0:T(8,128)(2,1)}, u32[]{:S(2)}, u32[]{:S(2)}) collective-permute-start(bf16[96,1536]{1,0:T(8,128)(2,1)S(1)} %collective-permute-done.4.refs_2_), channel_id=1, source_target_pairs={{16,0},{32,16},{48,32},{64,48},{80,64},{96,80},{112,96},{0,112},{1... | collective-permute-start | bytes 884744 | tf_op jit(solution)/shard_map/ppermute | solution.py:383
  16.8 0.7 copy-done.4
  17.5 0.0 collective-permute-done.3.refs_1_
  17.5 0.0 collective-permute-start.5
  17.5 0.7 copy-done.6
  18.2 5.6 %collective-permute-done.6.refs_4_ = bf16[96,1536]{1,0:T(8,128)(2,1)} collective-permute-done((bf16[96,1536]{1,0:T(8,128)(2,1)S(1)}, bf16[96,1536]{1,0:T(8,128)(2,1)}, u32[]{:S(2)}, u32[]{:S(2)}) %collective-permute-start.6) | collective-permute-done | bytes 294944 | tf_op jit(solution)/shard_map/ppermute | solution.py:383
  23.8 3.8 %collective-permute-start.8 = (bf16[96,1536]{1,0:T(8,128)(2,1)}, bf16[96,1536]{1,0:T(8,128)(2,1)S(1)}, u32[]{:S(2)}, u32[]{:S(2)}) collective-permute-start(bf16[96,1536]{1,0:T(8,128)(2,1)} %collective-permute-done.6.refs_4_), channel_id=1, source_target_pairs={{16,0},{32,16},{48,32},{64,48},{80,64},{96,80},{112,96},{0,112},{1... | collective-permute-start | bytes 884744 | tf_op jit(solution)/shard_map/ppermute | solution.py:383
  27.6 1.0 collective-permute-done.5.refs_3_
  28.6 0.0 collective-permute-start.7
  28.6 1.7 %constant_dynamic-slice_fusion = (bf16[128,768]{1,0:T(8,128)(2,1)}, bf16[128,768]{1,0:T(8,128)(2,1)S(1)}) fusion(bf16[128,1536]{1,0:T(8,128)(2,1)} %param.10, s32[]{:T(128)S(6)} %select_n.27, s32[]{:T(128)S(6)} %select_n.26), kind=kLoop, calls=%fused_computation.21 | loop fusion | bytes 786440 | tf_op jit(solution)/shard_map/dynamic_slice | solution.py:425
  30.4 0.1 pad_add_fusion.place_ref
  30.4 4.1 %collective-permute-done.8.refs_6_ = bf16[96,1536]{1,0:T(8,128)(2,1)S(1)} collective-permute-done((bf16[96,1536]{1,0:T(8,128)(2,1)}, bf16[96,1536]{1,0:T(8,128)(2,1)S(1)}, u32[]{:S(2)}, u32[]{:S(2)}) %collective-permute-start.8) | collective-permute-done | bytes 294944 | tf_op jit(solution)/shard_map/ppermute | solution.py:383
  34.6 3.7 %collective-permute-start.10 = (bf16[96,768]{1,0:T(8,128)(2,1)S(1)}, bf16[96,768]{1,0:T(8,128)(2,1)S(1)}, u32[]{:S(2)}, u32[]{:S(2)}) collective-permute-start(bf16[96,768]{1,0:T(8,128)(2,1)S(1)} %slice.39), channel_id=1, source_target_pairs={{16,0},{32,16},{48,32},{64,48},{80,64},{96,80},{112,96},{0,112},{1... | collective-permute-start | bytes 442376 | tf_op jit(solution)/shard_map/ppermute | solution.py:386
  38.2 0.9 collective-permute-done.7.refs_5_
  39.1 0.1 collective-permute-start.9
  39.2 0.0 copy-start.3
  39.3 0.0 copy-start.5
  39.3 0.0 copy-start.7
  39.3 3.2 %forward_own.1 = (f32[4,1,384]{2,1,0:T(1,128)S(1)}, f32[4,1,384]{2,1,0:T(1,128)S(1)}, f32[4,128,384]{2,1,0:T(8,128)S(1)}) custom-call(s32[4,27]{1,0:T(4,128)S(1)} %copy-done.8, bf16[4,384,128]{2,1,0:T(8,128)(2,1)S(1)} %bitcast.46, bf16[4,384,128]{2,1,0:T(8,128)(2,1)S(1)} %bitcast.39, bf16[4,384,128]{2,1,0:T(8,128)(2,1)S(1)} %bitcast.42, ...), custom_call_target="tpu_custom_call" | custom-call | flops 3000000000 | bytes 4000000 | tf_op jit(solution)/shard_map/forward_own/pallas_call | solution.py:292
  42.5 3.0 %collective-permute-done.9.refs_7_ = bf16[96,768]{1,0:T(8,128)(2,1)S(1)} collective-permute-done((bf16[96,768]{1,0:T(8,128)(2,1)S(1)}, bf16[96,768]{1,0:T(8,128)(2,1)S(1)}, u32[]{:S(2)}, u32[]{:S(2)}) %collective-permute-start.9) | collective-permute-done | bytes 147488 | tf_op jit(solution)/shard_map/ppermute | solution.py:386
  45.5 2.1 %back_parts.1 = (bf16[768,1536]{1,0:T(8,128)(2,1)S(1)}, bf16[128,1536]{1,0:T(8,128)(2,1)S(1)}, f32[128,1536]{1,0:T(8,128)S(1)}) custom-call(s32[3]{0:T(128)S(1)} %pad_add_fusion.place_ref, bf16[128,768]{1,0:T(8,128)(2,1)} %collective-permute-done.other_ref, bf16[128,768]{1,0:T(8,128)(2,1)S(1)} %get-tuple-element.64.mine_ref, bf16[96,1536]{1,0:T(8,128)(2,1)S(1)} %bitcast.55, ...), custom_call_target="tpu_custom_call" | custom-call | flops 2000000000 | bytes 4000000 | tf_op jit(solution)/shard_map/back_parts/pallas_call | solution.py:331
  47.6 0.9 collective-permute-start.12
  48.6 4.8 %forward_halo.1 = (bf16[4,384,128]{2,1,0:T(8,128)(2,1)S(1)}, bf16[4,128,384]{2,1,0:T(8,128)(2,1)S(1)}, f32[4,1,384]{2,1,0:T(1,128)S(1)}) custom-call(s32[4,27]{1,0:T(4,128)S(1)} %copy-done.8, bf16[4,384,128]{2,1,0:T(8,128)(2,1)S(1)} %bitcast.47, f32[4,1,384]{2,1,0:T(1,128)S(1)} %get-tuple-element.34.top_in, f32[4,1,384]{2,1,0:T(1,128)S(1)} %get-tuple-element.35.total_in, ...), custom_call_target="tpu_custom_call" | custom-call | flops 5000000000 | bytes 4000000 | tf_op jit(solution)/shard_map/forward_halo/pallas_call | solution.py:300
  53.4 1.5 %collective-permute-start.11 = (bf16[1536,128]{1,0:T(8,128)(2,1)S(1)}, bf16[1536,128]{1,0:T(8,128)(2,1)S(1)}, u32[]{:S(2)}, u32[]{:S(2)}) collective-permute-start(bf16[1536,128]{1,0:T(8,128)(2,1)S(1)} %bitcast.50), channel_id=1, source_target_pairs={{0,128},{128,0},{1,129},{129,1},{2,130},{130,2},{3,131},{131,3},{4... | collective-permute-start | bytes 1179656 | tf_op jit(solution)/shard_map/ppermute | solution.py:366
  54.8 2.0 %collective-permute-done.12.back_got_ref = bf16[128,1536]{1,0:T(8,128)(2,1)S(1)} collective-permute-done((bf16[128,1536]{1,0:T(8,128)(2,1)S(1)}, bf16[128,1536]{1,0:T(8,128)(2,1)S(1)}, u32[]{:S(2)}, u32[]{:S(2)}) %collective-permute-start.12) | collective-permute-done | bytes 393248 | tf_op jit(solution)/shard_map/ppermute | solution.py:366
  56.9 6.7 %backward_halo.1 = (bf16[2,4,384,128]{3,2,1,0:T(8,128)(2,1)S(1)}, bf16[2,4,384,128]{3,2,1,0:T(8,128)(2,1)S(1)}, f32[4,128,384]{2,1,0:T(8,128)S(1)}, bf16[4,128,384]{2,1,0:T(8,128)(2,1)S(1)}, f32[1,128]{1,0:T(1,128)S(1)}) custom-call(s32[4,27]{1,0:T(4,128)S(1)} %copy-done.8, bf16[4,384,128]{2,1,0:T(8,128)(2,1)S(1)} %bitcast.48, ...), custom_call_target="tpu_custom_call" | custom-call | flops 12000000000 | bytes 4000000 | tf_op jit(solution)/shard_map/backward_halo/pallas_call | solution.py:309
  63.6 1.0 collective-permute-done.11.got_ref.other_ref
  64.6 2.2 %projected_parts.1 = (bf16[96,1536]{1,0:T(8,128)(2,1)S(1)}, bf16[96,1536]{1,0:T(8,128)(2,1)S(1)}, bf16[96,1536]{1,0:T(8,128)(2,1)S(1)}, bf16[96,1536]{1,0:T(8,12...) custom-call(s32[3]{0:T(128)S(1)} %pad_add_fusion.place_ref, ...), custom_call_target="tpu_custom_call" | custom-call | flops 2000000000 | bytes 4000000 | tf_op jit(solution)/shard_map/projected_parts/pallas_call | solution.py:339
  66.8 0.1 collective-permute-start.13
  66.9 1.5 %weight_parts.1 = (bf16[2,2,2,96,128]{4,3,2,1,0:T(8,128)(2,1)S(1)}, f32[2,2,2,96,128]{4,3,2,1,0:T(8,128)S(1)}) custom-call(s32[3]{0:T(128)S(1)} %pad_add_fusion.place_ref, bf16[768,1536]{1,0:T(8,128)(2,1)S(1)} %get-tuple-element.60.grad_ref, bf16[1536,128]{1,0:T(8,128)(2,1)S(1)} %bitcast.52, bf16[1536,128]{1,0:T(8,128)(2,1)S(1)} %collective-permute-done.11.got_ref.other_ref, ...), custom_call_target="tpu_custom_call" | custom-call | flops 2000000000 | bytes 4000000 | tf_op jit(solution)/shard_map/weight_parts/pallas_call | solution.py:353
  68.4 3.2 %collective-permute-start.23 = (bf16[2,2,2,96,128]{4,3,2,1,0:T(8,128)(2,1)S(1)}, bf16[2,2,2,96,128]{4,3,2,1,0:T(8,128)(2,1)S(1)}, u32[]{:S(2)}, u32[]{:S(2)}) collective-permute-start(bf16[2,2,2,96,128]{4,3,2,1,0:T(8,128)(2,1)S(1)} %get-tuple-element.62), channel_id=1, source_target_pairs={{0,1},{1,0},{2,3},{3,2},{4,5},{5,4},{6,7},{7,6},{8,9},{9,8},{10,11... | collective-permute-start | bytes 589832 | tf_op jit(solution)/shard_map/ppermute | solution.py:447
  71.6 1.3 %collective-permute-start.16 = (bf16[2,4,384,128]{3,2,1,0:T(8,128)(2,1)S(1)}, bf16[2,4,384,128]{3,2,1,0:T(8,128)(2,1)S(1)}, u32[]{:S(2)}, u32[]{:S(2)}) collective-permute-start(bf16[2,4,384,128]{3,2,1,0:T(8,128)(2,1)S(1)} %get-tuple-element.49), channel_id=1, source_target_pairs={{1,0},{2,1},{3,2},{4,3},{5,4},{6,5},{7,6},{8,7},{9,8},{10,9},{11,1... | collective-permute-start | bytes 2359304 | tf_op jit(solution)/shard_map/ppermute | solution.py:362
  72.9 3.1 %collective-permute-start.17 = (bf16[2,4,384,128]{3,2,1,0:T(8,128)(2,1)S(1)}, bf16[2,4,384,128]{3,2,1,0:T(8,128)(2,1)S(1)}, u32[]{:S(2)}, u32[]{:S(2)}) collective-permute-start(bf16[2,4,384,128]{3,2,1,0:T(8,128)(2,1)S(1)} %get-tuple-element.50), channel_id=1, source_target_pairs={{0,1},{1,2},{2,3},{3,4},{4,5},{5,6},{6,7},{7,8},{8,9},{9,10},{10,1... | collective-permute-start | bytes 2359304 | tf_op jit(solution)/shard_map/ppermute | solution.py:362
  76.0 3.0 %collective-permute-start.19 = (bf16[96,768]{1,0:T(8,128)(2,1)S(1)}, bf16[96,768]{1,0:T(8,128)(2,1)S(1)}, u32[]{:S(2)}, u32[]{:S(2)}) collective-permute-start(bf16[96,768]{1,0:T(8,128)(2,1)S(1)} %get-tuple-element.53), channel_id=1, source_target_pairs={{16,0},{32,16},{48,32},{64,48},{80,64},{96,80},{112,96},{0,112},{1... | collective-permute-start | bytes 442376 | tf_op jit(solution)/shard_map/ppermute | solution.py:396
  79.1 0.1 collective-permute-start.14
  79.2 2.5 %collective-permute-done.19 = bf16[96,768]{1,0:T(8,128)(2,1)S(1)} collective-permute-done((bf16[96,768]{1,0:T(8,128)(2,1)S(1)}, bf16[96,768]{1,0:T(8,128)(2,1)S(1)}, u32[]{:S(2)}, u32[]{:S(2)}) %collective-permute-start.19) | collective-permute-done | bytes 147488 | tf_op jit(solution)/shard_map/ppermute | solution.py:396
  81.8 2.7 %collective-permute-start.24 = (bf16[2,2,96,128]{3,2,1,0:T(8,128)(2,1)S(1)}, bf16[2,2,96,128]{3,2,1,0:T(8,128)(2,1)S(1)}, u32[]{:S(2)}, u32[]{:S(2)}) collective-permute-start(bf16[2,2,96,128]{3,2,1,0:T(8,128)(2,1)S(1)} %fusion.2), channel_id=1, source_target_pairs={{0,2},{2,0},{1,3},{3,1},{4,6},{6,4},{5,7},{7,5},{8,10},{10,8},{9,1... | collective-permute-start | bytes 294920 | tf_op jit(solution)/shard_map/ppermute | solution.py:373
  84.5 3.8 %collective-permute-start.20 = (bf16[96,1536]{1,0:T(8,128)(2,1)S(1)}, bf16[96,1536]{1,0:T(8,128)(2,1)S(1)}, u32[]{:S(2)}, u32[]{:S(2)}) collective-permute-start(bf16[96,1536]{1,0:T(8,128)(2,1)S(1)} %pad_maximum_fusion.2), channel_id=1, source_target_pairs={{16,0},{32,16},{48,32},{64,48},{80,64},{96,80},{112,96},{0,112},{1... | collective-permute-start | bytes 884744 | tf_op jit(solution)/shard_map/ppermute | solution.py:405
  88.3 3.8 %collective-permute-done.24 = bf16[2,2,96,128]{3,2,1,0:T(8,128)(2,1)S(1)} collective-permute-done((bf16[2,2,96,128]{3,2,1,0:T(8,128)(2,1)S(1)}, bf16[2,2,96,128]{3,2,1,0:T(8,128)(2,1)S(1)}, u32[]{:S(2)}, u32[]{:S(2)}) %collective-permute-start.24) | collective-permute-done | bytes 98336 | tf_op jit(solution)/shard_map/ppermute | solution.py:373
  92.1 0.1 add_convert_fusion.4
  92.2 0.4 collective-permute-start.15
  92.6 1.1 collective-permute-done.20
  93.7 0.1 add_convert_fusion.2
  93.8 3.8 %collective-permute-start.21 = (bf16[96,1536]{1,0:T(8,128)(2,1)S(1)}, bf16[96,1536]{1,0:T(8,128)(2,1)S(1)}, u32[]{:S(2)}, u32[]{:S(2)}) collective-permute-start(bf16[96,1536]{1,0:T(8,128)(2,1)S(1)} %add_convert_fusion.2), channel_id=1, source_target_pairs={{16,0},{32,16},{48,32},{64,48},{80,64},{96,80},{112,96},{0,112},{1... | collective-permute-start | bytes 884744 | tf_op jit(solution)/shard_map/ppermute | solution.py:405
  97.5 6.2 %backward_own.1 = (bf16[4,384,128]{2,1,0:T(8,128)(2,1)}, bf16[4,384,128]{2,1,0:T(8,128)(2,1)}, bf16[4,384,128]{2,1,0:T(8,128)(2,1)}, f32[1,128]{1,0:T(1,128)S(1)}) custom-call(s32[4,27]{1,0:T(4,128)S(1)} %copy-done.8, bf16[4,384,128]{2,1,0:T(8,128)(2,1)S(1)} %bitcast.49, bf16[4,128,384]{2,1,0:T(8,128)(2,1)S(1)} %get-tuple-element.47.back_ref, ...), custom_call_target="tpu_custom_call" | custom-call | flops 6000000000 | bytes 4000000 | tf_op jit(solution)/shard_map/backward_own/pallas_call | solution.py:319
  103.8 0.1 add_convert_fusion.3
  103.9 0.1 collective-permute-start.18
  104.0 0.1 add_convert_fusion.1
  104.1 3.3 %collective-permute-start.22 = (bf16[96,1536]{1,0:T(8,128)(2,1)S(1)}, bf16[96,1536]{1,0:T(8,128)(2,1)S(1)}, u32[]{:S(2)}, u32[]{:S(2)}) collective-permute-start(bf16[96,1536]{1,0:T(8,128)(2,1)S(1)} %add_convert_fusion.1), channel_id=1, source_target_pairs={{16,0},{32,16},{48,32},{64,48},{80,64},{96,80},{112,96},{0,112},{1... | collective-permute-start | bytes 884744 | tf_op jit(solution)/shard_map/ppermute | solution.py:405
  107.4 11.2 %collective-permute-start.25 = (bf16[96,128]{1,0:T(8,128)(2,1)S(1)}, bf16[96,128]{1,0:T(8,128)(2,1)S(1)}, u32[]{:S(2)}, u32[]{:S(2)}) collective-permute-start(bf16[96,128]{1,0:T(8,128)(2,1)S(1)} %get-tuple-element.65), channel_id=1, source_target_pairs={{0,0},{4,4},{8,128},{12,132},{128,8},{132,12},{136,136},{140,140},... | collective-permute-start | bytes 73736 | tf_op jit(solution)/shard_map/ppermute | solution.py:457
  118.6 0.1 collective-permute-start.26
  118.7 0.1 collective-permute-start.27
  118.8 1.6 %collective-permute-done.25 = bf16[96,128]{1,0:T(8,128)(2,1)S(1)} collective-permute-done((bf16[96,128]{1,0:T(8,128)(2,1)S(1)}, bf16[96,128]{1,0:T(8,128)(2,1)S(1)}, u32[]{:S(2)}, u32[]{:S(2)}) %collective-permute-start.25) | collective-permute-done | bytes 24608 | tf_op jit(solution)/shard_map/ppermute | solution.py:457
  120.4 3.0 %collective-permute-start.28 = (bf16[96,128]{1,0:T(8,128)(2,1)S(1)}, bf16[96,128]{1,0:T(8,128)(2,1)S(1)}, u32[]{:S(2)}, u32[]{:S(2)}) collective-permute-start(bf16[96,128]{1,0:T(8,128)(2,1)S(1)} %get-tuple-element.66), channel_id=1, source_target_pairs={{0,132},{4,128},{8,4},{12,0},{128,140},{132,136},{136,12},{140,8},... | collective-permute-start | bytes 73736 | tf_op jit(solution)/shard_map/ppermute | solution.py:457
  123.4 1.2 collective-permute-done.26
  124.6 0.5 collective-permute-done.28
  125.1 0.6 add_bitcast_fusion
  125.8 0.8 fusion
  (40 shorter events, 0.3 us)
Async XLA Ops:
  0.6 38.6 %copy-start = (bf16[1,1536,128]{2,1,0:T(8,128)(2,1)S(1)}, bf16[1,1536,128]{2,1,0:T(8,128)(2,1)}, u32[]{:S(2)}) copy-start(bf16[1,1536,128]{2,1,0:T(8,128)(2,1)} %param.7) | copy-start | bytes 1179652
  0.6 38.6 %copy-start.1 = (bf16[1,1536,128]{2,1,0:T(8,128)(2,1)S(1)}, bf16[1,1536,128]{2,1,0:T(8,128)(2,1)}, u32[]{:S(2)}) copy-start(bf16[1,1536,128]{2,1,0:T(8,128)(2,1)} %param.8) | copy-start | bytes 1179652
  0.7 38.6 %copy-start.2 = (bf16[1,1536,128]{2,1,0:T(8,128)(2,1)S(1)}, bf16[1,1536,128]{2,1,0:T(8,128)(2,1)}, u32[]{:S(2)}) copy-start(bf16[1,1536,128]{2,1,0:T(8,128)(2,1)} %param.6) | copy-start | bytes 1179652
  0.7 38.6 %copy-start.8 = (s32[4,27]{1,0:T(4,128)S(1)}, s32[4,27]{1,0:T(4,128)}, u32[]{:S(2)}) copy-start(s32[4,27]{1,0:T(4,128)} %pattern_ref.7) | copy-start | bytes 1300
  0.7 12.5 %collective-permute-start.4 = (bf16[96,1536]{1,0:T(8,128)(2,1)}, bf16[96,1536]{1,0:T(8,128)(2,1)S(1)}, u32[]{:S(2)}, u32[]{:S(2)}) collective-permute-start(bf16[96,1536]{1,0:T(8,128)(2,1)} %bitcast.53), channel_id=1, source_target_pairs={{16,0},{32,16},{48,32},{64,48},{80,64},{96,80},{112,96},{0,112},{1... | collective-permute-start | bytes 884744 | tf_op jit(solution)/shard_map/ppermute | solution.py:383
  6.6 10.9 %collective-permute-start.3 = (bf16[96,1536]{1,0:T(8,128)(2,1)}, bf16[96,1536]{1,0:T(8,128)(2,1)S(1)}, u32[]{:S(2)}, u32[]{:S(2)}) collective-permute-start(bf16[96,1536]{1,0:T(8,128)(2,1)} %bitcast.54), channel_id=1, source_target_pairs={{0,16},{16,32},{32,48},{48,64},{64,80},{80,96},{96,112},{112,0},{1... | collective-permute-start | bytes 884744 | tf_op jit(solution)/shard_map/ppermute | solution.py:383
  8.7 30.5 %collective-permute-start.1 = (bf16[2,4,384,128]{3,2,1,0:T(8,128)(2,1)}, bf16[2,4,384,128]{3,2,1,0:T(8,128)(2,1)S(1)}, u32[]{:S(2)}, u32[]{:S(2)}) collective-permute-start(bf16[2,4,384,128]{3,2,1,0:T(8,128)(2,1)} %pad_maximum_fusion), channel_id=1, source_target_pairs={{0,1},{1,2},{2,3},{3,4},{4,5},{5,6},{6,7},{7,8},{8,9},{9,10},{10,1... | collective-permute-start | bytes 2359304 | tf_op jit(solution)/shard_map/ppermute | solution.py:362
  10.2 29.0 %collective-permute-start.2 = (bf16[2,4,384,128]{3,2,1,0:T(8,128)(2,1)}, bf16[2,4,384,128]{3,2,1,0:T(8,128)(2,1)S(1)}, u32[]{:S(2)}, u32[]{:S(2)}) collective-permute-start(bf16[2,4,384,128]{3,2,1,0:T(8,128)(2,1)} %pad_maximum_fusion), channel_id=1, source_target_pairs={{1,0},{2,1},{3,2},{4,3},{5,4},{6,5},{7,6},{8,7},{9,8},{10,9},{11,1... | collective-permute-start | bytes 2359304 | tf_op jit(solution)/shard_map/ppermute | solution.py:362
  13.2 10.6 %collective-permute-start.6 = (bf16[96,1536]{1,0:T(8,128)(2,1)S(1)}, bf16[96,1536]{1,0:T(8,128)(2,1)}, u32[]{:S(2)}, u32[]{:S(2)}) collective-permute-start(bf16[96,1536]{1,0:T(8,128)(2,1)S(1)} %collective-permute-done.4.refs_2_), channel_id=1, source_target_pairs={{16,0},{32,16},{48,32},{64,48},{80,64},{96,80},{112,96},{0,112},{1... | collective-permute-start | bytes 884744 | tf_op jit(solution)/shard_map/ppermute | solution.py:383
  16.8 0.7 copy-start.4
  17.5 11.1 %collective-permute-start.5 = (bf16[96,1536]{1,0:T(8,128)(2,1)S(1)}, bf16[96,1536]{1,0:T(8,128)(2,1)}, u32[]{:S(2)}, u32[]{:S(2)}) collective-permute-start(bf16[96,1536]{1,0:T(8,128)(2,1)S(1)} %collective-permute-done.3.refs_1_), channel_id=1, source_target_pairs={{0,16},{16,32},{32,48},{48,64},{64,80},{80,96},{96,112},{112,0},{1... | collective-permute-start | bytes 884744 | tf_op jit(solution)/shard_map/ppermute | solution.py:383
  17.5 0.7 copy-start.6
  23.8 10.7 %collective-permute-start.8 = (bf16[96,1536]{1,0:T(8,128)(2,1)}, bf16[96,1536]{1,0:T(8,128)(2,1)S(1)}, u32[]{:S(2)}, u32[]{:S(2)}) collective-permute-start(bf16[96,1536]{1,0:T(8,128)(2,1)} %collective-permute-done.6.refs_4_), channel_id=1, source_target_pairs={{16,0},{32,16},{48,32},{64,48},{80,64},{96,80},{112,96},{0,112},{1... | collective-permute-start | bytes 884744 | tf_op jit(solution)/shard_map/ppermute | solution.py:383
  28.6 10.4 %collective-permute-start.7 = (bf16[96,1536]{1,0:T(8,128)(2,1)}, bf16[96,1536]{1,0:T(8,128)(2,1)S(1)}, u32[]{:S(2)}, u32[]{:S(2)}) collective-permute-start(bf16[96,1536]{1,0:T(8,128)(2,1)} %collective-permute-done.5.refs_3_), channel_id=1, source_target_pairs={{0,16},{16,32},{32,48},{48,64},{64,80},{80,96},{96,112},{112,0},{1... | collective-permute-start | bytes 884744 | tf_op jit(solution)/shard_map/ppermute | solution.py:383
  30.4 12.1 %collective-permute-start = (bf16[128,768]{1,0:T(8,128)(2,1)}, bf16[128,768]{1,0:T(8,128)(2,1)}, u32[]{:S(2)}, u32[]{:S(2)}) collective-permute-start(bf16[128,768]{1,0:T(8,128)(2,1)} %get-tuple-element.63), channel_id=1, source_target_pairs={{0,128},{128,0},{1,129},{129,1},{2,130},{130,2},{3,131},{131,3},{4... | collective-permute-start | bytes 589832 | tf_op jit(solution)/shard_map/ppermute | solution.py:366
  34.6 7.9 %collective-permute-start.10 = (bf16[96,768]{1,0:T(8,128)(2,1)S(1)}, bf16[96,768]{1,0:T(8,128)(2,1)S(1)}, u32[]{:S(2)}, u32[]{:S(2)}) collective-permute-start(bf16[96,768]{1,0:T(8,128)(2,1)S(1)} %slice.39), channel_id=1, source_target_pairs={{16,0},{32,16},{48,32},{64,48},{80,64},{96,80},{112,96},{0,112},{1... | collective-permute-start | bytes 442376 | tf_op jit(solution)/shard_map/ppermute | solution.py:386
  39.1 6.4 %collective-permute-start.9 = (bf16[96,768]{1,0:T(8,128)(2,1)S(1)}, bf16[96,768]{1,0:T(8,128)(2,1)S(1)}, u32[]{:S(2)}, u32[]{:S(2)}) collective-permute-start(bf16[96,768]{1,0:T(8,128)(2,1)S(1)} %slice.38), channel_id=1, source_target_pairs={{0,16},{16,32},{32,48},{48,64},{64,80},{80,96},{96,112},{112,0},{1... | collective-permute-start | bytes 442376 | tf_op jit(solution)/shard_map/ppermute | solution.py:386
  39.2 6.3 %copy-start.3 = (bf16[1,1536,96]{1,2,0:T(8,128)(2,1)S(1)}, bf16[1,1536,96]{1,2,0:T(8,128)(2,1)}, u32[]{:S(2)}) copy-start(bf16[1,1536,96]{1,2,0:T(8,128)(2,1)} %param.9) | copy-start | bytes 884740
  39.3 6.3 %copy-start.5 = (bf16[96,1536]{1,0:T(8,128)(2,1)S(1)}, bf16[96,1536]{1,0:T(8,128)(2,1)}, u32[]{:S(2)}) copy-start(bf16[96,1536]{1,0:T(8,128)(2,1)} %copy-done.4) | copy-start | bytes 884740
  39.3 6.3 %copy-start.7 = (bf16[96,1536]{1,0:T(8,128)(2,1)S(1)}, bf16[96,1536]{1,0:T(8,128)(2,1)}, u32[]{:S(2)}) copy-start(bf16[96,1536]{1,0:T(8,128)(2,1)} %copy-done.6) | copy-start | bytes 884740
  47.6 9.2 %collective-permute-start.12 = (bf16[128,1536]{1,0:T(8,128)(2,1)S(1)}, bf16[128,1536]{1,0:T(8,128)(2,1)S(1)}, u32[]{:S(2)}, u32[]{:S(2)}) collective-permute-start(bf16[128,1536]{1,0:T(8,128)(2,1)S(1)} %get-tuple-element.37.early_ref), channel_id=1, source_target_pairs={{0,128},{128,0},{1,129},{129,1},{2,130},{130,2},{3,131},{131,3},{4... | collective-permute-start | bytes 1179656 | tf_op jit(solution)/shard_map/ppermute | solution.py:366
  53.4 11.2 %collective-permute-start.11 = (bf16[1536,128]{1,0:T(8,128)(2,1)S(1)}, bf16[1536,128]{1,0:T(8,128)(2,1)S(1)}, u32[]{:S(2)}, u32[]{:S(2)}) collective-permute-start(bf16[1536,128]{1,0:T(8,128)(2,1)S(1)} %bitcast.50), channel_id=1, source_target_pairs={{0,128},{128,0},{1,129},{129,1},{2,130},{130,2},{3,131},{131,3},{4... | collective-permute-start | bytes 1179656 | tf_op jit(solution)/shard_map/ppermute | solution.py:366
  66.8 12.3 %collective-permute-start.13 = (bf16[96,768]{1,0:T(8,128)(2,1)S(1)}, bf16[96,768]{1,0:T(8,128)(2,1)S(1)}, u32[]{:S(2)}, u32[]{:S(2)}) collective-permute-start(bf16[96,768]{1,0:T(8,128)(2,1)S(1)} %get-tuple-element.44), channel_id=1, source_target_pairs={{0,16},{16,32},{32,48},{48,64},{64,80},{80,96},{96,112},{112,0},{1... | collective-permute-start | bytes 442376 | tf_op jit(solution)/shard_map/ppermute | solution.py:395
  68.4 13.3 %collective-permute-start.23 = (bf16[2,2,2,96,128]{4,3,2,1,0:T(8,128)(2,1)S(1)}, bf16[2,2,2,96,128]{4,3,2,1,0:T(8,128)(2,1)S(1)}, u32[]{:S(2)}, u32[]{:S(2)}) collective-permute-start(bf16[2,2,2,96,128]{4,3,2,1,0:T(8,128)(2,1)S(1)} %get-tuple-element.62), channel_id=1, source_target_pairs={{0,1},{1,0},{2,3},{3,2},{4,5},{5,4},{6,7},{7,6},{8,9},{9,8},{10,11... | collective-permute-start | bytes 589832 | tf_op jit(solution)/shard_map/ppermute | solution.py:447
  71.6 25.9 %collective-permute-start.16 = (bf16[2,4,384,128]{3,2,1,0:T(8,128)(2,1)S(1)}, bf16[2,4,384,128]{3,2,1,0:T(8,128)(2,1)S(1)}, u32[]{:S(2)}, u32[]{:S(2)}) collective-permute-start(bf16[2,4,384,128]{3,2,1,0:T(8,128)(2,1)S(1)} %get-tuple-element.49), channel_id=1, source_target_pairs={{1,0},{2,1},{3,2},{4,3},{5,4},{6,5},{7,6},{8,7},{9,8},{10,9},{11,1... | collective-permute-start | bytes 2359304 | tf_op jit(solution)/shard_map/ppermute | solution.py:362
  72.9 24.6 %collective-permute-start.17 = (bf16[2,4,384,128]{3,2,1,0:T(8,128)(2,1)S(1)}, bf16[2,4,384,128]{3,2,1,0:T(8,128)(2,1)S(1)}, u32[]{:S(2)}, u32[]{:S(2)}) collective-permute-start(bf16[2,4,384,128]{3,2,1,0:T(8,128)(2,1)S(1)} %get-tuple-element.50), channel_id=1, source_target_pairs={{0,1},{1,2},{2,3},{3,4},{4,5},{5,6},{6,7},{7,8},{8,9},{9,10},{10,1... | collective-permute-start | bytes 2359304 | tf_op jit(solution)/shard_map/ppermute | solution.py:362
  76.0 5.7 %collective-permute-start.19 = (bf16[96,768]{1,0:T(8,128)(2,1)S(1)}, bf16[96,768]{1,0:T(8,128)(2,1)S(1)}, u32[]{:S(2)}, u32[]{:S(2)}) collective-permute-start(bf16[96,768]{1,0:T(8,128)(2,1)S(1)} %get-tuple-element.53), channel_id=1, source_target_pairs={{16,0},{32,16},{48,32},{64,48},{80,64},{96,80},{112,96},{0,112},{1... | collective-permute-start | bytes 442376 | tf_op jit(solution)/shard_map/ppermute | solution.py:396
  79.1 13.0 %collective-permute-start.14 = (bf16[96,1536]{1,0:T(8,128)(2,1)S(1)}, bf16[96,1536]{1,0:T(8,128)(2,1)S(1)}, u32[]{:S(2)}, u32[]{:S(2)}) collective-permute-start(bf16[96,1536]{1,0:T(8,128)(2,1)S(1)} %pad_maximum_fusion.1), channel_id=1, source_target_pairs={{0,16},{16,32},{32,48},{48,64},{64,80},{80,96},{96,112},{112,0},{1... | collective-permute-start | bytes 884744 | tf_op jit(solution)/shard_map/ppermute | solution.py:404
  81.8 10.3 %collective-permute-start.24 = (bf16[2,2,96,128]{3,2,1,0:T(8,128)(2,1)S(1)}, bf16[2,2,96,128]{3,2,1,0:T(8,128)(2,1)S(1)}, u32[]{:S(2)}, u32[]{:S(2)}) collective-permute-start(bf16[2,2,96,128]{3,2,1,0:T(8,128)(2,1)S(1)} %fusion.2), channel_id=1, source_target_pairs={{0,2},{2,0},{1,3},{3,1},{4,6},{6,4},{5,7},{7,5},{8,10},{10,8},{9,1... | collective-permute-start | bytes 294920 | tf_op jit(solution)/shard_map/ppermute | solution.py:373
  84.5 9.1 %collective-permute-start.20 = (bf16[96,1536]{1,0:T(8,128)(2,1)S(1)}, bf16[96,1536]{1,0:T(8,128)(2,1)S(1)}, u32[]{:S(2)}, u32[]{:S(2)}) collective-permute-start(bf16[96,1536]{1,0:T(8,128)(2,1)S(1)} %pad_maximum_fusion.2), channel_id=1, source_target_pairs={{16,0},{32,16},{48,32},{64,48},{80,64},{96,80},{112,96},{0,112},{1... | collective-permute-start | bytes 884744 | tf_op jit(solution)/shard_map/ppermute | solution.py:405
  92.2 11.6 %collective-permute-start.15 = (bf16[96,1536]{1,0:T(8,128)(2,1)S(1)}, bf16[96,1536]{1,0:T(8,128)(2,1)S(1)}, u32[]{:S(2)}, u32[]{:S(2)}) collective-permute-start(bf16[96,1536]{1,0:T(8,128)(2,1)S(1)} %add_convert_fusion.4), channel_id=1, source_target_pairs={{0,16},{16,32},{32,48},{48,64},{64,80},{80,96},{96,112},{112,0},{1... | collective-permute-start | bytes 884744 | tf_op jit(solution)/shard_map/ppermute | solution.py:404
  93.8 10.2 %collective-permute-start.21 = (bf16[96,1536]{1,0:T(8,128)(2,1)S(1)}, bf16[96,1536]{1,0:T(8,128)(2,1)S(1)}, u32[]{:S(2)}, u32[]{:S(2)}) collective-permute-start(bf16[96,1536]{1,0:T(8,128)(2,1)S(1)} %add_convert_fusion.2), channel_id=1, source_target_pairs={{16,0},{32,16},{48,32},{64,48},{80,64},{96,80},{112,96},{0,112},{1... | collective-permute-start | bytes 884744 | tf_op jit(solution)/shard_map/ppermute | solution.py:405
  103.9 21.9 %collective-permute-start.18 = (bf16[96,1536]{1,0:T(8,128)(2,1)S(1)}, bf16[96,1536]{1,0:T(8,128)(2,1)S(1)}, u32[]{:S(2)}, u32[]{:S(2)}) collective-permute-start(bf16[96,1536]{1,0:T(8,128)(2,1)S(1)} %add_convert_fusion.3), channel_id=1, source_target_pairs={{0,16},{16,32},{32,48},{48,64},{64,80},{80,96},{96,112},{112,0},{1... | collective-permute-start | bytes 884744 | tf_op jit(solution)/shard_map/ppermute | solution.py:404
  104.1 21.6 %collective-permute-start.22 = (bf16[96,1536]{1,0:T(8,128)(2,1)S(1)}, bf16[96,1536]{1,0:T(8,128)(2,1)S(1)}, u32[]{:S(2)}, u32[]{:S(2)}) collective-permute-start(bf16[96,1536]{1,0:T(8,128)(2,1)S(1)} %add_convert_fusion.1), channel_id=1, source_target_pairs={{16,0},{32,16},{48,32},{64,48},{80,64},{96,80},{112,96},{0,112},{1... | collective-permute-start | bytes 884744 | tf_op jit(solution)/shard_map/ppermute | solution.py:405
  107.4 13.0 %collective-permute-start.25 = (bf16[96,128]{1,0:T(8,128)(2,1)S(1)}, bf16[96,128]{1,0:T(8,128)(2,1)S(1)}, u32[]{:S(2)}, u32[]{:S(2)}) collective-permute-start(bf16[96,128]{1,0:T(8,128)(2,1)S(1)} %get-tuple-element.65), channel_id=1, source_target_pairs={{0,0},{4,4},{8,128},{12,132},{128,8},{132,12},{136,136},{140,140},... | collective-permute-start | bytes 73736 | tf_op jit(solution)/shard_map/ppermute | solution.py:457
  118.6 6.0 %collective-permute-start.26 = (bf16[96,128]{1,0:T(8,128)(2,1)S(1)}, bf16[96,128]{1,0:T(8,128)(2,1)S(1)}, u32[]{:S(2)}, u32[]{:S(2)}) collective-permute-start(bf16[96,128]{1,0:T(8,128)(2,1)S(1)} %get-tuple-element.68), channel_id=1, source_target_pairs={{0,4},{4,0},{8,132},{12,128},{128,12},{132,8},{136,140},{140,136},... | collective-permute-start | bytes 73736 | tf_op jit(solution)/shard_map/ppermute | solution.py:457
  118.7 5.9 %collective-permute-start.27 = (bf16[96,128]{1,0:T(8,128)(2,1)S(1)}, bf16[96,128]{1,0:T(8,128)(2,1)S(1)}, u32[]{:S(2)}, u32[]{:S(2)}) collective-permute-start(bf16[96,128]{1,0:T(8,128)(2,1)S(1)} %get-tuple-element.67), channel_id=1, source_target_pairs={{0,128},{4,132},{8,0},{12,4},{128,136},{132,140},{136,8},{140,12},... | collective-permute-start | bytes 73736 | tf_op jit(solution)/shard_map/ppermute | solution.py:457
  120.4 4.7 %collective-permute-start.28 = (bf16[96,128]{1,0:T(8,128)(2,1)S(1)}, bf16[96,128]{1,0:T(8,128)(2,1)S(1)}, u32[]{:S(2)}, u32[]{:S(2)}) collective-permute-start(bf16[96,128]{1,0:T(8,128)(2,1)S(1)} %get-tuple-element.66), channel_id=1, source_target_pairs={{0,132},{4,128},{8,4},{12,0},{128,140},{132,136},{136,12},{140,8},... | collective-permute-start | bytes 73736 | tf_op jit(solution)/shard_map/ppermute | solution.py:457

commit v2 on v1

--- a/solution.py
+++ b/solution.py
@@ -184,13 +184,12 @@
 
 def backward_own_kernel(
     pattern_ref, q_ref, back_ref, att_ref, lse_ref, k_ref, v_ref, dq_in, up_ref, down_ref,
-    dq_ref, dk_ref, dv_ref, zero_ref,
+    dq_ref, dk_ref, dv_ref,
     tile_of, place_of, p0, p1, d0, d1, delta, dq, dk, dv,
 ):
     count = build_pairs(pattern_ref, tile_of, place_of, (1,))
     dk[...] = up_ref[0].astype(F32) + down_ref[0].astype(F32)
     dv[...] = up_ref[1].astype(F32) + down_ref[1].astype(F32)
-    zero_ref[...] = jnp.zeros(zero_ref.shape, F32)
     dq[...] = dq_in[...]
     backward_pairs(
         count, q_ref, back_ref, att_ref, lse_ref, k_ref, v_ref, tile_of, place_of,
@@ -238,6 +237,10 @@
         block[...] = total[at(offset)]
     blocks[-2][...] = total[at(4), : tokens // 2]
     blocks[-1][...] = total[at(4), tokens // 2 :]
+
+
+def arrived_kernel(up_ref, down_ref, zero_ref):
+    zero_ref[...] = jnp.zeros(zero_ref.shape, F32)
 
 
 def weight_kernel(place_ref, grad_ref, att_ref, other_ref, early_ref, send_ref, keep_ref, heads, total):
@@ -315,7 +318,7 @@
 
 
 def backward_own(*args):
-    outs = [(BLOCK, BF), (BLOCK, BF), (BLOCK, BF), ((1, HDIM), F32)]
+    outs = [(BLOCK, BF), (BLOCK, BF), (BLOCK, BF)]
     return kernel_call(
         backward_own_kernel, "backward_own", outs, [SM] + [VM] * 9,
         PAIR_LISTS + TERMS
@@ -347,11 +350,15 @@
     )(place, w_mine, *args)
 
 
+def arrived(up, down):
+    return kernel_call(arrived_kernel, "arrived", [((1, HDIM), F32)], [ANY] * 2, [], 1000)(up, down)[0]
+
+
 def weight_parts(place, grad_half, att, att_other, early):
     feats, tokens = grad_half.shape
     shape = (2, 2, 2, feats // 8, HDIM)
     return kernel_call(
-        weight_kernel, "weight_parts", [(shape, BF), (shape, F32)], [SM] + [VM] * 3 + [HB],
+        weight_kernel, "weight_parts", [(shape, BF), (shape, F32)], [SM] + [VM] * 3 + [ANY],
         [pltpu.VMEM((tokens, 2 * HDIM), BF), pltpu.VMEM((feats, 2 * HDIM), F32)],
         2_000_000_000,
     )(place, grad_half, att, att_other, early)
@@ -392,7 +399,8 @@
     onward = [(i, (i + 1) % size) for i in range(size)]
     backward = [(j, i) for i, j in onward]
     middle = parts[-1].shape[1]
-    right = lax.ppermute(parts[-2], "z", onward).astype(F32)
+    first = lax.ppermute(parts[-2], "z", onward)
+    right = first.astype(F32)
     left = lax.ppermute(parts[-1], "z", backward).astype(F32)
     by_offset = {offset: part.astype(F32) for offset, part in zip(RING, parts)}
     last = size // 2 - 1
@@ -405,7 +413,7 @@
         left = lax.ppermute(left.astype(BF), "z", backward).astype(F32)
         if offset:
             right, left = right + by_offset[offset], left + by_offset[-offset]
-    return right + left + by_offset[0]
+    return right + left + by_offset[0], first
 
 
 def body(queries, key_rows, value_rows, out_grad, proj_weight, pattern):
@@ -436,14 +444,16 @@
         pattern, q, back_mine, back_got, att_flip, lse, above, below
     )
     up, down = shifted(up, -1), shifted(down, 1)
-    dq, dk, dv, late = backward_own(
+    late = arrived(up, down)
+    dq, dk, dv = backward_own(
         pattern, q, back, att_flip, lse, keys, values, dq_part, up, down
     )
 
     parts = projected_parts(place, w_mine, w_other, att, att_other, zero)
-    projected = ring_summed(parts, late[:, :1]).astype(BF).T[None]
-
-    sent, kept = weight_parts(place, grad_half, att, att_other, zero)
+    projected, first = ring_summed(parts, late[:, :1])
+    projected = projected.astype(BF).T[None]
+
+    sent, kept = weight_parts(place, grad_half, att, att_other, first)
     got = lax.ppermute(sent, "core", [(0, 1), (1, 0)])
     kept, got = halved(kept + got.astype(F32), "xh", 1, 2, 2, lax.axis_index("xh"))
 

time: 128 us -> 135 us (1.055)
  starting transfers between devices: 61.3 us -> 55.8 us
  local copies, waits for them, and re-layouts: 3.26 us -> 8.32 us
  waiting for transfers between devices: 30 us -> 34.7 us
  Pallas kernels: 26.8 us -> 30.1 us
    ppermute x4, starting transfers between devices: 14.4 us -> 7.38 us  [body(): summed = summed + lax.ppermute(piece, ('xl', 'y'), route).astype(F32)]
    ppermute x4, starting transfers between devices: 7.16 us -> 13.2 us  [shifted(): return lax.ppermute(block, ST, route)]
    unnamed x18 -> x44, local copies, waits for them, and re-layouts: 1.46 us -> 6.51 us
    ppermute x3, waiting for transfers between devices: 1.08 us -> 3.6 us  [ring_summed(): left = lax.ppermute(left.astype(BF), 'z', backward).astype(F32)]
    ppermute x1, waiting for transfers between devices: 2.48 us -> 0.01 us  [ring_summed(): left = lax.ppermute(parts[-1], 'z', backward).astype(F32)]
    ppermute x1, waiting for transfers between devices: 3.78 us -> 6.08 us  [halved(): return (keep, lax.ppermute(send, axis, route))]
    ppermute x3, waiting for transfers between devices: 11.4 us -> 13.7 us  [ring_gathered(): lax.ppermute(left, 'z', backward)]
    ppermute x1, starting transfers between devices: 2.7 us -> 0.64 us  [halved(): return (keep, lax.ppermute(send, axis, route))]
  transfers between devices with their start and end apart: 29 -> 29, of which waited for: 14 -> 14; matrix products, arithmetic and copies ran while one was open for 4% -> 4% of each run, Pallas kernels for 18% -> 19%
where the time goes in v2:
time: 135 us; the launch traced here: 134 us
  starting transfers between devices  55.8 us (41%)
  waiting for transfers between devices  34.7 us (26%)
  Pallas kernels  30.1 us (22%)
  local copies, waits for them, and re-layouts  8.32 us (6%)
  other arithmetic  4.21 us (3%)
    ppermute x3, waiting for transfers between devices, ring_gathered(): lax.ppermute(left, 'z', backward)  13.7 us
    ppermute x3, starting transfers between devices, ring_gathered(): lax.ppermute(left, 'z', backward)  13.3 us
    ppermute x4, starting transfers between devices, shifted(): return lax.ppermute(block, ST, route)  13.2 us
    ppermute x3, starting transfers between devices, ring_summed(): left = lax.ppermute(left.astype(BF), 'z', backward).astype(F32)  8.91 us
    pallas_call x1, Pallas kernels, backward_own(): kernel_call(backward_own_kernel, 'backward_own', outs, [SM] + [VM] * 9, P...  7.49 us
    ppermute x4, starting transfers between devices, body(): summed = summed + lax.ppermute(piece, ('xl', 'y'), route).astype(F32)  7.38 us
    pallas_call x1, Pallas kernels, backward_halo(): kernel_call(backward_halo_kernel, 'backward_halo', outs, [SM] + [VM] * 5...  6.68 us
    unnamed x44, local copies, waits for them, and re-layouts  6.51 us
  transfers between devices with their start and end apart: 29, of which 14 were waited for; matrix products, arithmetic and copies ran while one was open for 4% of the time, Pallas kernels for 19%

profile of v2, /device:TPU:2, one launch (start us, length us, event | category | flops | bytes accessed | tf_op | source)
XLA Modules:
  0.0 134.3 jit_solution(1922566309246634284)
XLA Ops:
  0.7 5.9 %collective-permute-start.4 = (bf16[96,1536]{1,0:T(8,128)(2,1)}, bf16[96,1536]{1,0:T(8,128)(2,1)S(1)}, u32[]{:S(2)}, u32[]{:S(2)}) collective-permute-start(bf16[96,1536]{1,0:T(8,128)(2,1)} %bitcast.53), channel_id=1, source_target_pairs={{16,0},{32,16},{48,32},{64,48},{80,64},{96,80},{112,96},{0,112},{1... | collective-permute-start | bytes 884744 | tf_op jit(solution)/shard_map/ppermute | solution.py:390
  6.6 2.1 %pad_maximum_fusion = bf16[2,4,384,128]{3,2,1,0:T(8,128)(2,1)} fusion(bf16[1,4,384,128]{3,2,1,0:T(8,128)(2,1)} %bitcast.41, bf16[1,4,384,128]{3,2,1,0:T(8,128)(2,1)} %bitcast.38), kind=kLoop, calls=%fused_computation | loop fusion | flops 393216 | bytes 1572864 | tf_op jit(solution)/shard_map/stack | solution.py:426
  8.7 1.5 %collective-permute-start.1 = (bf16[2,4,384,128]{3,2,1,0:T(8,128)(2,1)}, bf16[2,4,384,128]{3,2,1,0:T(8,128)(2,1)S(1)}, u32[]{:S(2)}, u32[]{:S(2)}) collective-permute-start(bf16[2,4,384,128]{3,2,1,0:T(8,128)(2,1)} %pad_maximum_fusion), channel_id=1, source_target_pairs={{0,1},{1,2},{2,3},{3,4},{4,5},{5,6},{6,7},{7,8},{8,9},{9,10},{10,1... | collective-permute-start | bytes 2359304 | tf_op jit(solution)/shard_map/ppermute | solution.py:369
  10.2 1.3 collective-permute-start.2
  11.5 1.7 %collective-permute-done.4.refs_2_ = bf16[96,1536]{1,0:T(8,128)(2,1)S(1)} collective-permute-done((bf16[96,1536]{1,0:T(8,128)(2,1)}, bf16[96,1536]{1,0:T(8,128)(2,1)S(1)}, u32[]{:S(2)}, u32[]{:S(2)}) %collective-permute-start.4) | collective-permute-done | bytes 294944 | tf_op jit(solution)/shard_map/ppermute | solution.py:390
  13.2 3.6 %collective-permute-start.6 = (bf16[96,1536]{1,0:T(8,128)(2,1)S(1)}, bf16[96,1536]{1,0:T(8,128)(2,1)}, u32[]{:S(2)}, u32[]{:S(2)}) collective-permute-start(bf16[96,1536]{1,0:T(8,128)(2,1)S(1)} %collective-permute-done.4.refs_2_), channel_id=1, source_target_pairs={{16,0},{32,16},{48,32},{64,48},{80,64},{96,80},{112,96},{0,112},{1... | collective-permute-start | bytes 884744 | tf_op jit(solution)/shard_map/ppermute | solution.py:390
  16.8 7.1 %collective-permute-done.6.refs_4_ = bf16[96,1536]{1,0:T(8,128)(2,1)} collective-permute-done((bf16[96,1536]{1,0:T(8,128)(2,1)S(1)}, bf16[96,1536]{1,0:T(8,128)(2,1)}, u32[]{:S(2)}, u32[]{:S(2)}) %collective-permute-start.6) | collective-permute-done | bytes 294944 | tf_op jit(solution)/shard_map/ppermute | solution.py:390
  23.9 3.8 %collective-permute-start.8 = (bf16[96,1536]{1,0:T(8,128)(2,1)}, bf16[96,1536]{1,0:T(8,128)(2,1)S(1)}, u32[]{:S(2)}, u32[]{:S(2)}) collective-permute-start(bf16[96,1536]{1,0:T(8,128)(2,1)} %collective-permute-done.6.refs_4_), channel_id=1, source_target_pairs={{16,0},{32,16},{48,32},{64,48},{80,64},{96,80},{112,96},{0,112},{1... | collective-permute-start | bytes 884744 | tf_op jit(solution)/shard_map/ppermute | solution.py:390
  27.7 0.2 collective-permute-done.5.refs_3_
  27.9 1.7 %constant_dynamic-slice_fusion = (bf16[128,768]{1,0:T(8,128)(2,1)}, bf16[128,768]{1,0:T(8,128)(2,1)S(1)}) fusion(bf16[128,1536]{1,0:T(8,128)(2,1)} %param.10, s32[]{:T(128)S(6)} %select_n.27, s32[]{:T(128)S(6)} %select_n.26), kind=kLoop, calls=%fused_computation.21 | loop fusion | bytes 786440 | tf_op jit(solution)/shard_map/dynamic_slice | solution.py:433
  29.6 0.1 pad_add_fusion.place_ref
  29.7 4.9 %collective-permute-done.8.refs_6_ = bf16[96,1536]{1,0:T(8,128)(2,1)S(1)} collective-permute-done((bf16[96,1536]{1,0:T(8,128)(2,1)}, bf16[96,1536]{1,0:T(8,128)(2,1)S(1)}, u32[]{:S(2)}, u32[]{:S(2)}) %collective-permute-start.8) | collective-permute-done | bytes 294944 | tf_op jit(solution)/shard_map/ppermute | solution.py:390
  34.6 3.7 %collective-permute-start.10 = (bf16[96,768]{1,0:T(8,128)(2,1)S(1)}, bf16[96,768]{1,0:T(8,128)(2,1)S(1)}, u32[]{:S(2)}, u32[]{:S(2)}) collective-permute-start(bf16[96,768]{1,0:T(8,128)(2,1)S(1)} %slice.39), channel_id=1, source_target_pairs={{16,0},{32,16},{48,32},{64,48},{80,64},{96,80},{112,96},{0,112},{1... | collective-permute-start | bytes 442376 | tf_op jit(solution)/shard_map/ppermute | solution.py:393
  38.2 0.1 collective-permute-done.7.refs_5_
  38.4 0.1 collective-permute-start.9
  38.5 0.0 copy-start.11
  38.5 4.0 %forward_own.1 = (f32[4,1,384]{2,1,0:T(1,128)S(1)}, f32[4,1,384]{2,1,0:T(1,128)S(1)}, f32[4,128,384]{2,1,0:T(8,128)S(1)}) custom-call(s32[4,27]{1,0:T(4,128)S(1)} %copy-done.13, bf16[4,384,128]{2,1,0:T(8,128)(2,1)S(1)} %bitcast.46, bf16[4,384,128]{2,1,0:T(8,128)(2,1)S(1)} %bitcast.39, bf16[4,384,128]{2,1,0:T(8,128)(2,1)S(1)} %bitcast.42, ...), custom_call_target="tpu_custom_call" | custom-call | flops 3000000000 | bytes 4000000 | tf_op jit(solution)/shard_map/forward_own/pallas_call | solution.py:295
  42.6 2.2 %collective-permute-done.9.refs_7_ = bf16[96,768]{1,0:T(8,128)(2,1)S(1)} collective-permute-done((bf16[96,768]{1,0:T(8,128)(2,1)S(1)}, bf16[96,768]{1,0:T(8,128)(2,1)S(1)}, u32[]{:S(2)}, u32[]{:S(2)}) %collective-permute-start.9) | collective-permute-done | bytes 147488 | tf_op jit(solution)/shard_map/ppermute | solution.py:393
  44.8 2.2 %back_parts.1 = (bf16[768,1536]{1,0:T(8,128)(2,1)S(1)}, bf16[128,1536]{1,0:T(8,128)(2,1)S(1)}, f32[128,1536]{1,0:T(8,128)S(1)}) custom-call(s32[3]{0:T(128)S(1)} %pad_add_fusion.place_ref, bf16[128,768]{1,0:T(8,128)(2,1)} %collective-permute-done.other_ref, bf16[128,768]{1,0:T(8,128)(2,1)S(1)} %get-tuple-element.62.mine_ref, bf16[96,1536]{1,0:T(8,128)(2,1)S(1)} %bitcast.55, ...), custom_call_target="tpu_custom_call" | custom-call | flops 2000000000 | bytes 4000000 | tf_op jit(solution)/shard_map/back_parts/pallas_call | solution.py:334
  47.0 1.4 %copy-done.14 = bf16[768,1536]{1,0:T(8,128)(2,1)} copy-done((bf16[768,1536]{1,0:T(8,128)(2,1)}, bf16[768,1536]{1,0:T(8,128)(2,1)S(1)}, u32[]{:S(2)}) %copy-start.14) | copy-done | bytes 2359320
  48.4 0.9 collective-permute-start.12
  49.2 5.2 %forward_halo.1 = (bf16[4,384,128]{2,1,0:T(8,128)(2,1)S(1)}, bf16[4,128,384]{2,1,0:T(8,128)(2,1)S(1)}, f32[4,1,384]{2,1,0:T(1,128)S(1)}) custom-call(s32[4,27]{1,0:T(4,128)S(1)} %copy-done.13, bf16[4,384,128]{2,1,0:T(8,128)(2,1)S(1)} %bitcast.47, f32[4,1,384]{2,1,0:T(1,128)S(1)} %get-tuple-element.33.top_in, f32[4,1,384]{2,1,0:T(1,128)S(1)} %get-tuple-element.34.total_in, ...), custom_call_target="tpu_custom_call" | custom-call | flops 5000000000 | bytes 4000000 | tf_op jit(solution)/shard_map/forward_halo/pallas_call | solution.py:303
  54.4 0.0 copy-start.18
  54.4 0.0 copy-start.7
  54.4 1.4 %collective-permute-start.11 = (bf16[1536,128]{1,0:T(8,128)(2,1)S(1)}, bf16[1536,128]{1,0:T(8,128)(2,1)S(1)}, u32[]{:S(2)}, u32[]{:S(2)}) collective-permute-start(bf16[1536,128]{1,0:T(8,128)(2,1)S(1)} %bitcast.50), channel_id=1, source_target_pairs={{0,128},{128,0},{1,129},{129,1},{2,130},{130,2},{3,131},{131,3},{4... | collective-permute-start | bytes 1179656 | tf_op jit(solution)/shard_map/ppermute | solution.py:373
  55.9 1.7 %collective-permute-done.12.back_got_ref = bf16[128,1536]{1,0:T(8,128)(2,1)S(1)} collective-permute-done((bf16[128,1536]{1,0:T(8,128)(2,1)S(1)}, bf16[128,1536]{1,0:T(8,128)(2,1)S(1)}, u32[]{:S(2)}, u32[]{:S(2)}) %collective-permute-start.12) | collective-permute-done | bytes 393248 | tf_op jit(solution)/shard_map/ppermute | solution.py:373
  57.6 6.7 %backward_halo.1 = (bf16[2,4,384,128]{3,2,1,0:T(8,128)(2,1)S(1)}, bf16[2,4,384,128]{3,2,1,0:T(8,128)(2,1)S(1)}, f32[4,128,384]{2,1,0:T(8,128)S(1)}, bf16[4,128,384]{2,1,0:T(8,128)(2,1)S(1)}, f32[1,128]{1,0:T(1,128)S(1)}) custom-call(s32[4,27]{1,0:T(4,128)S(1)} %copy-done.13, bf16[4,384,128]{2,1,0:T(8,128)(2,1)S(1)} %bitcast.48, ...), custom_call_target="tpu_custom_call" | custom-call | flops 12000000000 | bytes 4000000 | tf_op jit(solution)/shard_map/backward_halo/pallas_call | solution.py:312
  64.3 0.0 copy-start.20
  64.3 0.7 copy-done.20
  65.1 3.1 %projected_parts.1 = (bf16[96,1536]{1,0:T(8,128)(2,1)S(1)}, bf16[96,1536]{1,0:T(8,128)(2,1)S(1)}, bf16[96,1536]{1,0:T(8,128)(2,1)S(1)}, bf16[96,1536]{1,0:T(8,12...) custom-call(s32[3]{0:T(128)S(1)} %pad_add_fusion.place_ref, ...), custom_call_target="tpu_custom_call" | custom-call | flops 2000000000 | bytes 4000000 | tf_op jit(solution)/shard_map/projected_parts/pallas_call | solution.py:342
  68.2 0.7 copy-done.12
  68.8 1.3 collective-permute-start.16
  70.1 9.2 %collective-permute-start.17 = (bf16[2,4,384,128]{3,2,1,0:T(8,128)(2,1)}, bf16[2,4,384,128]{3,2,1,0:T(8,128)(2,1)S(1)}, u32[]{:S(2)}, u32[]{:S(2)}) collective-permute-start(bf16[2,4,384,128]{3,2,1,0:T(8,128)(2,1)} %copy-done.2), channel_id=1, source_target_pairs={{0,1},{1,2},{2,3},{3,4},{4,5},{5,6},{6,7},{7,8},{8,9},{9,10},{10,1... | collective-permute-start | bytes 2359304 | tf_op jit(solution)/shard_map/ppermute | solution.py:369
  79.3 3.0 %collective-permute-start.19 = (bf16[96,768]{1,0:T(8,128)(2,1)}, bf16[96,768]{1,0:T(8,128)(2,1)S(1)}, u32[]{:S(2)}, u32[]{:S(2)}) collective-permute-start(bf16[96,768]{1,0:T(8,128)(2,1)} %copy-done.12), channel_id=1, source_target_pairs={{16,0},{32,16},{48,32},{64,48},{80,64},{96,80},{112,96},{0,112},{1... | collective-permute-start | bytes 442376 | tf_op jit(solution)/shard_map/ppermute | solution.py:404
  82.4 0.0 copy-start.8
  82.4 1.0 copy-done.8
  83.4 1.0 copy-done.10
  84.3 1.7 %copy-done.15 = bf16[768,1536]{1,0:T(8,128)(2,1)S(1)} copy-done((bf16[768,1536]{1,0:T(8,128)(2,1)S(1)}, bf16[768,1536]{1,0:T(8,128)(2,1)}, u32[]{:S(2)}) %copy-start.15) | copy-done | bytes 2359320
  86.0 1.5 %weight_parts.1 = (bf16[2,2,2,96,128]{4,3,2,1,0:T(8,128)(2,1)S(1)}, f32[2,2,2,96,128]{4,3,2,1,0:T(8,128)S(1)}) custom-call(s32[3]{0:T(128)S(1)} %pad_add_fusion.place_ref, bf16[768,1536]{1,0:T(8,128)(2,1)S(1)} %copy-done.15, bf16[1536,128]{1,0:T(8,128)(2,1)S(1)} %bitcast.52, bf16[1536,128]{1,0:T(8,128)(2,1)S(1)} %copy-done.10, ...), custom_call_target="tpu_custom_call" | custom-call | flops 2000000000 | bytes 4000000 | tf_op jit(solution)/shard_map/weight_parts/pallas_call | solution.py:360
  87.6 3.0 %collective-permute-start.23 = (bf16[2,2,2,96,128]{4,3,2,1,0:T(8,128)(2,1)S(1)}, bf16[2,2,2,96,128]{4,3,2,1,0:T(8,128)(2,1)S(1)}, u32[]{:S(2)}, u32[]{:S(2)}) collective-permute-start(bf16[2,2,2,96,128]{4,3,2,1,0:T(8,128)(2,1)S(1)} %get-tuple-element.60), channel_id=1, source_target_pairs={{0,1},{1,0},{2,3},{3,2},{4,5},{5,4},{6,7},{7,6},{8,9},{9,8},{10,11... | collective-permute-start | bytes 589832 | tf_op jit(solution)/shard_map/ppermute | solution.py:457
  90.6 0.1 collective-permute-start.14
  90.8 0.9 collective-permute-done.23
  91.7 0.6 collective-permute-start.24
  92.4 2.1 %collective-permute-start.20 = (bf16[96,1536]{1,0:T(8,128)(2,1)S(1)}, bf16[96,1536]{1,0:T(8,128)(2,1)S(1)}, u32[]{:S(2)}, u32[]{:S(2)}) collective-permute-start(bf16[96,1536]{1,0:T(8,128)(2,1)S(1)} %pad_maximum_fusion.2), channel_id=1, source_target_pairs={{16,0},{32,16},{48,32},{64,48},{80,64},{96,80},{112,96},{0,112},{1... | collective-permute-start | bytes 884744 | tf_op jit(solution)/shard_map/ppermute | solution.py:413
  94.5 6.1 %collective-permute-done.24 = bf16[2,2,96,128]{3,2,1,0:T(8,128)(2,1)S(1)} collective-permute-done((bf16[2,2,96,128]{3,2,1,0:T(8,128)(2,1)S(1)}, bf16[2,2,96,128]{3,2,1,0:T(8,128)(2,1)S(1)}, u32[]{:S(2)}, u32[]{:S(2)}) %collective-permute-start.24) | collective-permute-done | bytes 98336 | tf_op jit(solution)/shard_map/ppermute | solution.py:380
  100.6 2.9 %collective-permute-start.25 = (bf16[96,128]{1,0:T(8,128)(2,1)S(1)}, bf16[96,128]{1,0:T(8,128)(2,1)S(1)}, u32[]{:S(2)}, u32[]{:S(2)}) collective-permute-start(bf16[96,128]{1,0:T(8,128)(2,1)S(1)} %get-tuple-element.63), channel_id=1, source_target_pairs={{0,0},{4,4},{8,128},{12,132},{128,8},{132,12},{136,136},{140,140},... | collective-permute-start | bytes 73736 | tf_op jit(solution)/shard_map/ppermute | solution.py:467
  103.6 4.1 %collective-permute-start.26 = (bf16[96,128]{1,0:T(8,128)(2,1)S(1)}, bf16[96,128]{1,0:T(8,128)(2,1)S(1)}, u32[]{:S(2)}, u32[]{:S(2)}) collective-permute-start(bf16[96,128]{1,0:T(8,128)(2,1)S(1)} %get-tuple-element.66), channel_id=1, source_target_pairs={{0,4},{4,0},{8,132},{12,128},{128,12},{132,8},{136,140},{140,136},... | collective-permute-start | bytes 73736 | tf_op jit(solution)/shard_map/ppermute | solution.py:467
  107.6 0.1 add_convert_fusion.4
  107.7 0.1 collective-permute-start.15
  107.8 0.9 collective-permute-done.25
  108.7 0.9 collective-permute-done.26
  109.6 0.4 collective-permute-start.28
  110.0 0.1 add_convert_fusion.2
  110.1 2.5 %collective-permute-done.27 = bf16[96,128]{1,0:T(8,128)(2,1)S(1)} collective-permute-done((bf16[96,128]{1,0:T(8,128)(2,1)S(1)}, bf16[96,128]{1,0:T(8,128)(2,1)S(1)}, u32[]{:S(2)}, u32[]{:S(2)}) %collective-permute-start.27) | collective-permute-done | bytes 24608 | tf_op jit(solution)/shard_map/ppermute | solution.py:467
  112.6 3.0 %collective-permute-start.21 = (bf16[96,1536]{1,0:T(8,128)(2,1)S(1)}, bf16[96,1536]{1,0:T(8,128)(2,1)S(1)}, u32[]{:S(2)}, u32[]{:S(2)}) collective-permute-start(bf16[96,1536]{1,0:T(8,128)(2,1)S(1)} %add_convert_fusion.2), channel_id=1, source_target_pairs={{16,0},{32,16},{48,32},{64,48},{80,64},{96,80},{112,96},{0,112},{1... | collective-permute-start | bytes 884744 | tf_op jit(solution)/shard_map/ppermute | solution.py:413
  115.6 0.6 add_bitcast_fusion
  116.3 2.0 %collective-permute-done.15 = bf16[96,1536]{1,0:T(8,128)(2,1)S(1)} collective-permute-done((bf16[96,1536]{1,0:T(8,128)(2,1)S(1)}, bf16[96,1536]{1,0:T(8,128)(2,1)S(1)}, u32[]{:S(2)}, u32[]{:S(2)}) %collective-permute-start.15) | collective-permute-done | bytes 294944 | tf_op jit(solution)/shard_map/ppermute | solution.py:412
  118.3 0.1 add_convert_fusion.3
  118.4 0.1 collective-permute-start.18
  118.5 3.6 %collective-permute-done.21 = bf16[96,1536]{1,0:T(8,128)(2,1)S(1)} collective-permute-done((bf16[96,1536]{1,0:T(8,128)(2,1)S(1)}, bf16[96,1536]{1,0:T(8,128)(2,1)S(1)}, u32[]{:S(2)}, u32[]{:S(2)}) %collective-permute-start.21) | collective-permute-done | bytes 294944 | tf_op jit(solution)/shard_map/ppermute | solution.py:413
  122.1 0.1 add_convert_fusion.1
  122.2 3.8 %collective-permute-start.22 = (bf16[96,1536]{1,0:T(8,128)(2,1)S(1)}, bf16[96,1536]{1,0:T(8,128)(2,1)S(1)}, u32[]{:S(2)}, u32[]{:S(2)}) collective-permute-start(bf16[96,1536]{1,0:T(8,128)(2,1)S(1)} %add_convert_fusion.1), channel_id=1, source_target_pairs={{16,0},{32,16},{48,32},{64,48},{80,64},{96,80},{112,96},{0,112},{1... | collective-permute-start | bytes 884744 | tf_op jit(solution)/shard_map/ppermute | solution.py:413
  126.0 7.5 %backward_own.1 = (bf16[4,384,128]{2,1,0:T(8,128)(2,1)}, bf16[4,384,128]{2,1,0:T(8,128)(2,1)}, bf16[4,384,128]{2,1,0:T(8,128)(2,1)}) custom-call(s32[4,27]{1,0:T(4,128)S(1)} %copy-done.13, bf16[4,384,128]{2,1,0:T(8,128)(2,1)S(1)} %bitcast.49, bf16[4,128,384]{2,1,0:T(8,128)(2,1)S(1)} %copy-done.21, bf16[4,128,384]{2,1,0:T(8,128)(2,1)S(1)} %copy-done.19, ...), custom_call_target="tpu_custom_call" | custom-call | flops 6000000000 | bytes 4000000 | tf_op jit(solution)/shard_map/backward_own/pallas_call | solution.py:322
  133.5 0.8 fusion
  (67 shorter events, 0.4 us)
Async XLA Ops:
  0.6 37.9 %copy-start = (bf16[1,1536,128]{2,1,0:T(8,128)(2,1)S(1)}, bf16[1,1536,128]{2,1,0:T(8,128)(2,1)}, u32[]{:S(2)}) copy-start(bf16[1,1536,128]{2,1,0:T(8,128)(2,1)} %param.7) | copy-start | bytes 1179652
  0.6 37.9 %copy-start.1 = (bf16[1,1536,128]{2,1,0:T(8,128)(2,1)S(1)}, bf16[1,1536,128]{2,1,0:T(8,128)(2,1)}, u32[]{:S(2)}) copy-start(bf16[1,1536,128]{2,1,0:T(8,128)(2,1)} %param.8) | copy-start | bytes 1179652
  0.7 37.9 %copy-start.6 = (bf16[1,1536,128]{2,1,0:T(8,128)(2,1)S(1)}, bf16[1,1536,128]{2,1,0:T(8,128)(2,1)}, u32[]{:S(2)}) copy-start(bf16[1,1536,128]{2,1,0:T(8,128)(2,1)} %param.6) | copy-start | bytes 1179652
  0.7 37.9 %copy-start.13 = (s32[4,27]{1,0:T(4,128)S(1)}, s32[4,27]{1,0:T(4,128)}, u32[]{:S(2)}) copy-start(s32[4,27]{1,0:T(4,128)} %pattern_ref.7) | copy-start | bytes 1300
  0.7 12.5 %collective-permute-start.4 = (bf16[96,1536]{1,0:T(8,128)(2,1)}, bf16[96,1536]{1,0:T(8,128)(2,1)S(1)}, u32[]{:S(2)}, u32[]{:S(2)}) collective-permute-start(bf16[96,1536]{1,0:T(8,128)(2,1)} %bitcast.53), channel_id=1, source_target_pairs={{16,0},{32,16},{48,32},{64,48},{80,64},{96,80},{112,96},{0,112},{1... | collective-permute-start | bytes 884744 | tf_op jit(solution)/shard_map/ppermute | solution.py:390
  6.6 10.2 %collective-permute-start.3 = (bf16[96,1536]{1,0:T(8,128)(2,1)}, bf16[96,1536]{1,0:T(8,128)(2,1)S(1)}, u32[]{:S(2)}, u32[]{:S(2)}) collective-permute-start(bf16[96,1536]{1,0:T(8,128)(2,1)} %bitcast.54), channel_id=1, source_target_pairs={{0,16},{16,32},{32,48},{48,64},{64,80},{80,96},{96,112},{112,0},{1... | collective-permute-start | bytes 884744 | tf_op jit(solution)/shard_map/ppermute | solution.py:390
  8.7 29.7 %collective-permute-start.1 = (bf16[2,4,384,128]{3,2,1,0:T(8,128)(2,1)}, bf16[2,4,384,128]{3,2,1,0:T(8,128)(2,1)S(1)}, u32[]{:S(2)}, u32[]{:S(2)}) collective-permute-start(bf16[2,4,384,128]{3,2,1,0:T(8,128)(2,1)} %pad_maximum_fusion), channel_id=1, source_target_pairs={{0,1},{1,2},{2,3},{3,4},{4,5},{5,6},{6,7},{7,8},{8,9},{9,10},{10,1... | collective-permute-start | bytes 2359304 | tf_op jit(solution)/shard_map/ppermute | solution.py:369
  10.2 28.3 %collective-permute-start.2 = (bf16[2,4,384,128]{3,2,1,0:T(8,128)(2,1)}, bf16[2,4,384,128]{3,2,1,0:T(8,128)(2,1)}, u32[]{:S(2)}, u32[]{:S(2)}) collective-permute-start(bf16[2,4,384,128]{3,2,1,0:T(8,128)(2,1)} %pad_maximum_fusion), channel_id=1, source_target_pairs={{1,0},{2,1},{3,2},{4,3},{5,4},{6,5},{7,6},{8,7},{9,8},{10,9},{11,1... | collective-permute-start | bytes 2359304 | tf_op jit(solution)/shard_map/ppermute | solution.py:369
  13.2 10.7 %collective-permute-start.6 = (bf16[96,1536]{1,0:T(8,128)(2,1)S(1)}, bf16[96,1536]{1,0:T(8,128)(2,1)}, u32[]{:S(2)}, u32[]{:S(2)}) collective-permute-start(bf16[96,1536]{1,0:T(8,128)(2,1)S(1)} %collective-permute-done.4.refs_2_), channel_id=1, source_target_pairs={{16,0},{32,16},{48,32},{64,48},{80,64},{96,80},{112,96},{0,112},{1... | collective-permute-start | bytes 884744 | tf_op jit(solution)/shard_map/ppermute | solution.py:390
  16.8 11.1 %collective-permute-start.5 = (bf16[96,1536]{1,0:T(8,128)(2,1)S(1)}, bf16[96,1536]{1,0:T(8,128)(2,1)}, u32[]{:S(2)}, u32[]{:S(2)}) collective-permute-start(bf16[96,1536]{1,0:T(8,128)(2,1)S(1)} %collective-permute-done.3.refs_1_), channel_id=1, source_target_pairs={{0,16},{16,32},{32,48},{48,64},{64,80},{80,96},{96,112},{112,0},{1... | collective-permute-start | bytes 884744 | tf_op jit(solution)/shard_map/ppermute | solution.py:390
  23.9 10.7 %collective-permute-start.8 = (bf16[96,1536]{1,0:T(8,128)(2,1)}, bf16[96,1536]{1,0:T(8,128)(2,1)S(1)}, u32[]{:S(2)}, u32[]{:S(2)}) collective-permute-start(bf16[96,1536]{1,0:T(8,128)(2,1)} %collective-permute-done.6.refs_4_), channel_id=1, source_target_pairs={{16,0},{32,16},{48,32},{64,48},{80,64},{96,80},{112,96},{0,112},{1... | collective-permute-start | bytes 884744 | tf_op jit(solution)/shard_map/ppermute | solution.py:390
  27.9 10.4 %collective-permute-start.7 = (bf16[96,1536]{1,0:T(8,128)(2,1)}, bf16[96,1536]{1,0:T(8,128)(2,1)S(1)}, u32[]{:S(2)}, u32[]{:S(2)}) collective-permute-start(bf16[96,1536]{1,0:T(8,128)(2,1)} %collective-permute-done.5.refs_3_), channel_id=1, source_target_pairs={{0,16},{16,32},{32,48},{48,64},{64,80},{80,96},{96,112},{112,0},{1... | collective-permute-start | bytes 884744 | tf_op jit(solution)/shard_map/ppermute | solution.py:390
  29.6 13.0 %collective-permute-start = (bf16[128,768]{1,0:T(8,128)(2,1)}, bf16[128,768]{1,0:T(8,128)(2,1)}, u32[]{:S(2)}, u32[]{:S(2)}) collective-permute-start(bf16[128,768]{1,0:T(8,128)(2,1)} %get-tuple-element.61), channel_id=1, source_target_pairs={{0,128},{128,0},{1,129},{129,1},{2,130},{130,2},{3,131},{131,3},{4... | collective-permute-start | bytes 589832 | tf_op jit(solution)/shard_map/ppermute | solution.py:373
  34.6 8.0 %collective-permute-start.10 = (bf16[96,768]{1,0:T(8,128)(2,1)S(1)}, bf16[96,768]{1,0:T(8,128)(2,1)S(1)}, u32[]{:S(2)}, u32[]{:S(2)}) collective-permute-start(bf16[96,768]{1,0:T(8,128)(2,1)S(1)} %slice.39), channel_id=1, source_target_pairs={{16,0},{32,16},{48,32},{64,48},{80,64},{96,80},{112,96},{0,112},{1... | collective-permute-start | bytes 442376 | tf_op jit(solution)/shard_map/ppermute | solution.py:393
  38.4 6.4 %collective-permute-start.9 = (bf16[96,768]{1,0:T(8,128)(2,1)S(1)}, bf16[96,768]{1,0:T(8,128)(2,1)S(1)}, u32[]{:S(2)}, u32[]{:S(2)}) collective-permute-start(bf16[96,768]{1,0:T(8,128)(2,1)S(1)} %slice.38), channel_id=1, source_target_pairs={{0,16},{16,32},{32,48},{48,64},{64,80},{80,96},{96,112},{112,0},{1... | collective-permute-start | bytes 442376 | tf_op jit(solution)/shard_map/ppermute | solution.py:393
  38.5 4.1 %copy-start.4 = (bf16[2,4,384,128]{3,2,1,0:T(8,128)(2,1)}, bf16[2,4,384,128]{3,2,1,0:T(8,128)(2,1)S(1)}, u32[]{:S(2)}) copy-start(bf16[2,4,384,128]{3,2,1,0:T(8,128)(2,1)S(1)} %collective-permute-done.1.e0.above_ref) | copy-start | bytes 2359300
  38.5 6.3 %copy-start.11 = (bf16[1,1536,96]{1,2,0:T(8,128)(2,1)S(1)}, bf16[1,1536,96]{1,2,0:T(8,128)(2,1)}, u32[]{:S(2)}) copy-start(bf16[1,1536,96]{1,2,0:T(8,128)(2,1)} %param.9) | copy-start | bytes 884740
  44.8 4.4 %copy-start.5 = (bf16[2,4,384,128]{3,2,1,0:T(8,128)(2,1)S(1)}, bf16[2,4,384,128]{3,2,1,0:T(8,128)(2,1)}, u32[]{:S(2)}) copy-start(bf16[2,4,384,128]{3,2,1,0:T(8,128)(2,1)} %copy-done.4) | copy-start | bytes 2359300
  47.0 1.4 %copy-start.14 = (bf16[768,1536]{1,0:T(8,128)(2,1)}, bf16[768,1536]{1,0:T(8,128)(2,1)S(1)}, u32[]{:S(2)}) copy-start(bf16[768,1536]{1,0:T(8,128)(2,1)S(1)} %get-tuple-element.58.grad_ref) | copy-start | bytes 7077892
  48.4 9.2 %collective-permute-start.12 = (bf16[128,1536]{1,0:T(8,128)(2,1)S(1)}, bf16[128,1536]{1,0:T(8,128)(2,1)S(1)}, u32[]{:S(2)}, u32[]{:S(2)}) collective-permute-start(bf16[128,1536]{1,0:T(8,128)(2,1)S(1)} %get-tuple-element.36.early_ref), channel_id=1, source_target_pairs={{0,128},{128,0},{1,129},{129,1},{2,130},{130,2},{3,131},{131,3},{4... | collective-permute-start | bytes 1179656 | tf_op jit(solution)/shard_map/ppermute | solution.py:373
  54.4 9.9 %copy-start.18 = (bf16[4,128,384]{2,1,0:T(8,128)(2,1)}, bf16[4,128,384]{2,1,0:T(8,128)(2,1)S(1)}, u32[]{:S(2)}) copy-start(bf16[4,128,384]{2,1,0:T(8,128)(2,1)S(1)} %get-tuple-element.39.att_ref) | copy-start | bytes 1179652
  54.4 10.6 %copy-start.7 = (bf16[4,384,128]{2,1,0:T(8,128)(2,1)}, bf16[4,384,128]{2,1,0:T(8,128)(2,1)S(1)}, u32[]{:S(2)}) copy-start(bf16[4,384,128]{2,1,0:T(8,128)(2,1)S(1)} %get-tuple-element.37) | copy-start | bytes 1179652
  54.4 10.6 %collective-permute-start.11 = (bf16[1536,128]{1,0:T(8,128)(2,1)S(1)}, bf16[1536,128]{1,0:T(8,128)(2,1)S(1)}, u32[]{:S(2)}, u32[]{:S(2)}) collective-permute-start(bf16[1536,128]{1,0:T(8,128)(2,1)S(1)} %bitcast.50), channel_id=1, source_target_pairs={{0,128},{128,0},{1,129},{129,1},{2,130},{130,2},{3,131},{131,3},{4... | collective-permute-start | bytes 1179656 | tf_op jit(solution)/shard_map/ppermute | solution.py:373
  64.3 0.7 copy-start.20
  65.0 3.1 %copy-start.2 = (bf16[2,4,384,128]{3,2,1,0:T(8,128)(2,1)}, bf16[2,4,384,128]{3,2,1,0:T(8,128)(2,1)S(1)}, u32[]{:S(2)}) copy-start(bf16[2,4,384,128]{3,2,1,0:T(8,128)(2,1)S(1)} %get-tuple-element.47) | copy-start | bytes 2359300
  65.0 3.1 %copy-start.3 = (bf16[2,4,384,128]{3,2,1,0:T(8,128)(2,1)}, bf16[2,4,384,128]{3,2,1,0:T(8,128)(2,1)S(1)}, u32[]{:S(2)}) copy-start(bf16[2,4,384,128]{3,2,1,0:T(8,128)(2,1)S(1)} %get-tuple-element.46) | copy-start | bytes 2359300
  65.0 3.1 %copy-start.16 = (f32[4,128,384]{2,1,0:T(8,128)}, f32[4,128,384]{2,1,0:T(8,128)S(1)}, u32[]{:S(2)}) copy-start(f32[4,128,384]{2,1,0:T(8,128)S(1)} %get-tuple-element.54.dq_in) | copy-start | bytes 2359300
  65.0 3.1 %copy-start.9 = (bf16[1536,128]{1,0:T(8,128)(2,1)}, bf16[1536,128]{1,0:T(8,128)(2,1)S(1)}, u32[]{:S(2)}) copy-start(bf16[1536,128]{1,0:T(8,128)(2,1)S(1)} %collective-permute-done.11.got_ref.other_ref) | copy-start | bytes 1179652
  68.1 0.7 copy-start.12
  68.8 13.5 %collective-permute-start.13 = (bf16[96,768]{1,0:T(8,128)(2,1)}, bf16[96,768]{1,0:T(8,128)(2,1)S(1)}, u32[]{:S(2)}, u32[]{:S(2)}) collective-permute-start(bf16[96,768]{1,0:T(8,128)(2,1)} %get-tuple-element.43), channel_id=1, source_target_pairs={{0,16},{16,32},{32,48},{48,64},{64,80},{80,96},{96,112},{112,0},{1... | collective-permute-start | bytes 442376 | tf_op jit(solution)/shard_map/ppermute | solution.py:402
  68.8 47.4 %collective-permute-start.16 = (bf16[2,4,384,128]{3,2,1,0:T(8,128)(2,1)}, bf16[2,4,384,128]{3,2,1,0:T(8,128)(2,1)S(1)}, u32[]{:S(2)}, u32[]{:S(2)}) collective-permute-start(bf16[2,4,384,128]{3,2,1,0:T(8,128)(2,1)} %copy-done.3), channel_id=1, source_target_pairs={{1,0},{2,1},{3,2},{4,3},{5,4},{6,5},{7,6},{8,7},{9,8},{10,9},{11,1... | collective-permute-start | bytes 2359304 | tf_op jit(solution)/shard_map/ppermute | solution.py:369
  70.1 46.1 %collective-permute-start.17 = (bf16[2,4,384,128]{3,2,1,0:T(8,128)(2,1)}, bf16[2,4,384,128]{3,2,1,0:T(8,128)(2,1)S(1)}, u32[]{:S(2)}, u32[]{:S(2)}) collective-permute-start(bf16[2,4,384,128]{3,2,1,0:T(8,128)(2,1)} %copy-done.2), channel_id=1, source_target_pairs={{0,1},{1,2},{2,3},{3,4},{4,5},{5,6},{6,7},{7,8},{8,9},{9,10},{10,1... | collective-permute-start | bytes 2359304 | tf_op jit(solution)/shard_map/ppermute | solution.py:369
  79.3 11.4 %collective-permute-start.19 = (bf16[96,768]{1,0:T(8,128)(2,1)}, bf16[96,768]{1,0:T(8,128)(2,1)S(1)}, u32[]{:S(2)}, u32[]{:S(2)}) collective-permute-start(bf16[96,768]{1,0:T(8,128)(2,1)} %copy-done.12), channel_id=1, source_target_pairs={{16,0},{32,16},{48,32},{64,48},{80,64},{96,80},{112,96},{0,112},{1... | collective-permute-start | bytes 442376 | tf_op jit(solution)/shard_map/ppermute | solution.py:404
  82.4 1.0 copy-start.8
  83.4 1.0 copy-start.10
  84.3 1.7 %copy-start.15 = (bf16[768,1536]{1,0:T(8,128)(2,1)S(1)}, bf16[768,1536]{1,0:T(8,128)(2,1)}, u32[]{:S(2)}) copy-start(bf16[768,1536]{1,0:T(8,128)(2,1)} %copy-done.14) | copy-start | bytes 7077892
  87.6 4.1 %collective-permute-start.23 = (bf16[2,2,2,96,128]{4,3,2,1,0:T(8,128)(2,1)S(1)}, bf16[2,2,2,96,128]{4,3,2,1,0:T(8,128)(2,1)S(1)}, u32[]{:S(2)}, u32[]{:S(2)}) collective-permute-start(bf16[2,2,2,96,128]{4,3,2,1,0:T(8,128)(2,1)S(1)} %get-tuple-element.60), channel_id=1, source_target_pairs={{0,1},{1,0},{2,3},{3,2},{4,5},{5,4},{6,7},{7,6},{8,9},{9,8},{10,11... | collective-permute-start | bytes 589832 | tf_op jit(solution)/shard_map/ppermute | solution.py:457
  90.6 12.9 %collective-permute-start.14 = (bf16[96,1536]{1,0:T(8,128)(2,1)S(1)}, bf16[96,1536]{1,0:T(8,128)(2,1)S(1)}, u32[]{:S(2)}, u32[]{:S(2)}) collective-permute-start(bf16[96,1536]{1,0:T(8,128)(2,1)S(1)} %pad_maximum_fusion.1), channel_id=1, source_target_pairs={{0,16},{16,32},{32,48},{48,64},{64,80},{80,96},{96,112},{112,0},{1... | collective-permute-start | bytes 884744 | tf_op jit(solution)/shard_map/ppermute | solution.py:412
  91.7 8.8 %collective-permute-start.24 = (bf16[2,2,96,128]{3,2,1,0:T(8,128)(2,1)S(1)}, bf16[2,2,96,128]{3,2,1,0:T(8,128)(2,1)S(1)}, u32[]{:S(2)}, u32[]{:S(2)}) collective-permute-start(bf16[2,2,96,128]{3,2,1,0:T(8,128)(2,1)S(1)} %fusion.2), channel_id=1, source_target_pairs={{0,2},{2,0},{1,3},{3,1},{4,6},{6,4},{5,7},{7,5},{8,10},{10,8},{9,1... | collective-permute-start | bytes 294920 | tf_op jit(solution)/shard_map/ppermute | solution.py:380
  92.4 15.3 %collective-permute-start.20 = (bf16[96,1536]{1,0:T(8,128)(2,1)S(1)}, bf16[96,1536]{1,0:T(8,128)(2,1)S(1)}, u32[]{:S(2)}, u32[]{:S(2)}) collective-permute-start(bf16[96,1536]{1,0:T(8,128)(2,1)S(1)} %pad_maximum_fusion.2), channel_id=1, source_target_pairs={{16,0},{32,16},{48,32},{64,48},{80,64},{96,80},{112,96},{0,112},{1... | collective-permute-start | bytes 884744 | tf_op jit(solution)/shard_map/ppermute | solution.py:413
  100.6 8.1 %collective-permute-start.25 = (bf16[96,128]{1,0:T(8,128)(2,1)S(1)}, bf16[96,128]{1,0:T(8,128)(2,1)S(1)}, u32[]{:S(2)}, u32[]{:S(2)}) collective-permute-start(bf16[96,128]{1,0:T(8,128)(2,1)S(1)} %get-tuple-element.63), channel_id=1, source_target_pairs={{0,0},{4,4},{8,128},{12,132},{128,8},{132,12},{136,136},{140,140},... | collective-permute-start | bytes 73736 | tf_op jit(solution)/shard_map/ppermute | solution.py:467
  103.6 6.0 %collective-permute-start.26 = (bf16[96,128]{1,0:T(8,128)(2,1)S(1)}, bf16[96,128]{1,0:T(8,128)(2,1)S(1)}, u32[]{:S(2)}, u32[]{:S(2)}) collective-permute-start(bf16[96,128]{1,0:T(8,128)(2,1)S(1)} %get-tuple-element.66), channel_id=1, source_target_pairs={{0,4},{4,0},{8,132},{12,128},{128,12},{132,8},{136,140},{140,136},... | collective-permute-start | bytes 73736 | tf_op jit(solution)/shard_map/ppermute | solution.py:467
  107.7 10.5 %collective-permute-start.15 = (bf16[96,1536]{1,0:T(8,128)(2,1)S(1)}, bf16[96,1536]{1,0:T(8,128)(2,1)S(1)}, u32[]{:S(2)}, u32[]{:S(2)}) collective-permute-start(bf16[96,1536]{1,0:T(8,128)(2,1)S(1)} %add_convert_fusion.4), channel_id=1, source_target_pairs={{0,16},{16,32},{32,48},{48,64},{64,80},{80,96},{96,112},{112,0},{1... | collective-permute-start | bytes 884744 | tf_op jit(solution)/shard_map/ppermute | solution.py:412
  108.7 3.8 %collective-permute-start.27 = (bf16[96,128]{1,0:T(8,128)(2,1)S(1)}, bf16[96,128]{1,0:T(8,128)(2,1)S(1)}, u32[]{:S(2)}, u32[]{:S(2)}) collective-permute-start(bf16[96,128]{1,0:T(8,128)(2,1)S(1)} %get-tuple-element.65), channel_id=1, source_target_pairs={{0,128},{4,132},{8,0},{12,4},{128,136},{132,140},{136,8},{140,12},... | collective-permute-start | bytes 73736 | tf_op jit(solution)/shard_map/ppermute | solution.py:467
  109.6 6.0 %collective-permute-start.28 = (bf16[96,128]{1,0:T(8,128)(2,1)S(1)}, bf16[96,128]{1,0:T(8,128)(2,1)S(1)}, u32[]{:S(2)}, u32[]{:S(2)}) collective-permute-start(bf16[96,128]{1,0:T(8,128)(2,1)S(1)} %get-tuple-element.64), channel_id=1, source_target_pairs={{0,132},{4,128},{8,4},{12,0},{128,140},{132,136},{136,12},{140,8},... | collective-permute-start | bytes 73736 | tf_op jit(solution)/shard_map/ppermute | solution.py:467
  112.6 9.5 %collective-permute-start.21 = (bf16[96,1536]{1,0:T(8,128)(2,1)S(1)}, bf16[96,1536]{1,0:T(8,128)(2,1)S(1)}, u32[]{:S(2)}, u32[]{:S(2)}) collective-permute-start(bf16[96,1536]{1,0:T(8,128)(2,1)S(1)} %add_convert_fusion.2), channel_id=1, source_target_pairs={{16,0},{32,16},{48,32},{64,48},{80,64},{96,80},{112,96},{0,112},{1... | collective-permute-start | bytes 884744 | tf_op jit(solution)/shard_map/ppermute | solution.py:413
  116.2 9.7 %copy-start.17 = (f32[4,128,384]{2,1,0:T(8,128)S(1)}, f32[4,128,384]{2,1,0:T(8,128)}, u32[]{:S(2)}) copy-start(f32[4,128,384]{2,1,0:T(8,128)} %copy-done.16) | copy-start | bytes 2359300
  116.2 9.7 %copy-start.19 = (bf16[4,128,384]{2,1,0:T(8,128)(2,1)S(1)}, bf16[4,128,384]{2,1,0:T(8,128)(2,1)}, u32[]{:S(2)}) copy-start(bf16[4,128,384]{2,1,0:T(8,128)(2,1)} %copy-done.18) | copy-start | bytes 1179652
  116.2 9.7 %copy-start.21 = (bf16[4,128,384]{2,1,0:T(8,128)(2,1)S(1)}, bf16[4,128,384]{2,1,0:T(8,128)(2,1)}, u32[]{:S(2)}) copy-start(bf16[4,128,384]{2,1,0:T(8,128)(2,1)} %copy-done.20) | copy-start | bytes 1179652
  118.4 15.1 %collective-permute-start.18 = (bf16[96,1536]{1,0:T(8,128)(2,1)S(1)}, bf16[96,1536]{1,0:T(8,128)(2,1)S(1)}, u32[]{:S(2)}, u32[]{:S(2)}) collective-permute-start(bf16[96,1536]{1,0:T(8,128)(2,1)S(1)} %add_convert_fusion.3), channel_id=1, source_target_pairs={{0,16},{16,32},{32,48},{48,64},{64,80},{80,96},{96,112},{112,0},{1... | collective-permute-start | bytes 884744 | tf_op jit(solution)/shard_map/ppermute | solution.py:412
  122.2 11.3 %collective-permute-start.22 = (bf16[96,1536]{1,0:T(8,128)(2,1)S(1)}, bf16[96,1536]{1,0:T(8,128)(2,1)S(1)}, u32[]{:S(2)}, u32[]{:S(2)}) collective-permute-start(bf16[96,1536]{1,0:T(8,128)(2,1)S(1)} %add_convert_fusion.1), channel_id=1, source_target_pairs={{16,0},{32,16},{48,32},{64,48},{80,64},{96,80},{112,96},{0,112},{1... | collective-permute-start | bytes 884744 | tf_op jit(solution)/shard_map/ppermute | solution.py:413
